TPU v7x, 256 devices: a whole 4x4x8 slice. The times are simulated.
256 devices in a mesh: seq: 64 (over z, x, core), head: 4 (over y).
Axes of the slice: x: 4, y: 4, z: 8, core: 2. Of those that a mesh axis runs over, the one named last changes fastest.
Arguments:
- queries: bfloat16 [49152, 2048], P('seq', 'head'), may hold values from -6 to 6
- attn_keys: bfloat16 [49152, 2048], P('seq', 'head'), may hold values from -6 to 6
- attn_values: bfloat16 [49152, 2048], P('seq', 'head'), may hold values from -36 to 36
- out_weight: bfloat16 [2048, 2048], P('head'), may hold values from -0.125 to 0.125
- grad_out: bfloat16 [49152, 2048], P('seq', 'head'), may hold values from -6 to 6
- drop_seed: int32 [1], replicated, may hold values from 0 to 32748
Outputs:
- output: bfloat16 [49152, 2048], P('seq', 'head')
- grad_queries: bfloat16 [49152, 2048], P('seq', 'head')
- grad_keys: bfloat16 [49152, 2048], P('seq', 'head')
- grad_values: bfloat16 [49152, 2048], P('seq', 'head')
- grad_weight: bfloat16 [2048, 2048], P('head')
All inputs are finite; a program needn't handle non-finite values.
Results may differ from a plain program's by a relative error of at most 0.023.
Values may be sent and summed in bfloat16 or wider, within the bound.
A program may use at most 128 MiB of HBM per device.

v0:
```python
import math

import jax
import jax.numpy as jnp
from jax import lax
from jax.sharding import PartitionSpec as P

HD = 128
SPAN = 256


eps_norm = 1e-05
keep_scale = 1.0 / 0.9


def prefix(value, axis, combine, identity, reverse):
    peers, position = (lax.axis_size(axis), lax.axis_index(axis))
    everything = lax.all_gather(value.astype(jnp.bfloat16), axis)
    start = jnp.broadcast_to(jnp.asarray(identity, value.dtype), value.shape)

    def hop(k, before):
        at = peers - 1 - k if reverse else k
        reached = at > position if reverse else at < position
        new = combine(before, everything[at].astype(value.dtype))
        return jnp.where(reached, new, before)

    return lax.fori_loop(0, peers, hop, start)


def keep_table(drop_seed, positions, features):
    seed_value = drop_seed[0]
    mixing = (positions * 181 + features * 227 + seed_value) % 32749
    hashed = (mixing * mixing % 32749 * 173 + mixing * 59 + features * 13 + positions * 7) % 32749
    return hashed % 10 != 0


def earlier_sum(blocks):
    return jnp.concatenate([jnp.zeros_like(blocks[:1]), jnp.cumsum(blocks[:-1], axis=0)], axis=0)


def later_sum(blocks):
    flipped = jnp.cumsum(jnp.flip(blocks[1:], 0), axis=0)
    return jnp.concatenate([jnp.flip(flipped, 0), jnp.zeros_like(blocks[:1])], axis=0)


def add_states(earlier, later):
    return earlier + later


def local(queries, attn_keys, attn_values, out_weight, grad_out, drop_seed):
    tok_rows, local_width = queries.shape
    local_heads = local_width // HD
    n_blocks = tok_rows // SPAN

    def split(array):
        return array.reshape(n_blocks, SPAN, local_heads, HD)

    query_blocks = split(queries)
    key_blocks = split(attn_keys)
    value_blocks = split(attn_values)
    causal = jnp.tril(jnp.ones((SPAN, SPAN), dtype=bool))[None, None]
    block_state = jnp.einsum(
        "cshi,cshj->chij", key_blocks, value_blocks, preferred_element_type=jnp.float32
    )
    shard_state = jnp.sum(block_state, axis=0)
    carried = prefix(shard_state, "seq", add_states, jnp.zeros_like(shard_state), False)
    state_b16 = (carried[None] + earlier_sum(block_state)).astype(jnp.bfloat16)
    inter = jnp.einsum(
        "cthi,chij->cthj", query_blocks, state_b16, preferred_element_type=jnp.float32
    )
    scores = jnp.einsum(
        "cthi,cshi->chts", query_blocks, key_blocks, preferred_element_type=jnp.float32
    )
    causal_scores = jnp.where(causal, scores, 0.0).astype(jnp.bfloat16)
    intra = jnp.einsum(
        "chts,cshj->cthj", causal_scores, value_blocks, preferred_element_type=jnp.float32
    )
    mixed = inter + intra
    inv_rms = 1.0 / jnp.sqrt(jnp.mean(mixed * mixed, axis=-1, keepdims=True) + eps_norm)
    normed = (mixed * inv_rms).astype(jnp.bfloat16).reshape(tok_rows, local_width)
    partial_value = jnp.dot(normed, out_weight, preferred_element_type=jnp.float32)
    projected = lax.psum_scatter(
        partial_value.astype(jnp.bfloat16), "head", scatter_dimension=1, tiled=True
    ).astype(jnp.float32)
    own_width = projected.shape[1]
    positions = lax.axis_index("seq") * tok_rows + jnp.arange(tok_rows, dtype=jnp.int32)
    features = lax.axis_index("head") * own_width + jnp.arange(own_width, dtype=jnp.int32)
    keep = keep_table(drop_seed, positions[:, None], features[None, :])
    output = jnp.where(keep, projected * keep_scale, 0.0).astype(jnp.bfloat16)
    grad_proj = jnp.where(keep, grad_out.astype(jnp.float32) * keep_scale, 0.0).astype(jnp.bfloat16)
    piece = lax.all_gather(grad_proj, "head", axis=1, tiled=True)
    grad_normed = lax.dot_general(
        piece, out_weight, (((1,), (1,)), ((), ())), preferred_element_type=jnp.float32
    )
    term = lax.dot_general(
        normed, piece, (((0,), (0,)), ((), ())), preferred_element_type=jnp.float32
    )
    weight_term = term
    grad_normed, weight_term = (grad_normed, weight_term)
    grad_scale = 1.0 / math.sqrt(tok_rows * lax.axis_size("seq"))
    summed = lax.psum(weight_term, "seq")
    grad_weight = (summed * grad_scale).astype(jnp.bfloat16)
    grad_blocks = grad_normed.reshape(n_blocks, SPAN, local_heads, HD)
    grad_mixed = (
        inv_rms
        * (
            grad_blocks
            - mixed * inv_rms * inv_rms * jnp.mean(grad_blocks * mixed, axis=-1, keepdims=True)
        )
    ).astype(jnp.bfloat16)
    block_grad = jnp.einsum(
        "cthi,cthj->chij", query_blocks, grad_mixed, preferred_element_type=jnp.float32
    )
    shard_grad = jnp.sum(block_grad, axis=0)
    arriving = prefix(shard_grad, "seq", add_states, jnp.zeros_like(shard_grad), True)
    suffix_b16 = (arriving[None] + later_sum(block_grad)).astype(jnp.bfloat16)
    grad_scores = jnp.einsum(
        "cthj,cshj->chts", grad_mixed, value_blocks, preferred_element_type=jnp.float32
    )
    grad_scores = jnp.where(causal, grad_scores, 0.0).astype(jnp.bfloat16)
    grad_query = jnp.einsum(
        "cthj,chij->cthi", grad_mixed, state_b16, preferred_element_type=jnp.float32
    ) + jnp.einsum("chts,cshi->cthi", grad_scores, key_blocks, preferred_element_type=jnp.float32)
    grad_key = jnp.einsum(
        "cshj,chij->cshi", value_blocks, suffix_b16, preferred_element_type=jnp.float32
    ) + jnp.einsum("chts,cthi->cshi", grad_scores, query_blocks, preferred_element_type=jnp.float32)
    grad_value = jnp.einsum(
        "cshi,chij->cshj", key_blocks, suffix_b16, preferred_element_type=jnp.float32
    ) + jnp.einsum("chts,cthj->cshj", causal_scores, grad_mixed, preferred_element_type=jnp.float32)
    grad_query = grad_query.astype(jnp.bfloat16).reshape(tok_rows, local_width)
    grad_key = grad_key.astype(jnp.bfloat16).reshape(tok_rows, local_width)
    grad_value = grad_value.astype(jnp.bfloat16).reshape(tok_rows, local_width)
    return (output, grad_query, grad_key, grad_value, grad_weight)


def solution(mesh):
    in_specs = (
        P("seq", "head"),
        P("seq", "head"),
        P("seq", "head"),
        P("head", None),
        P("seq", "head"),
        P(),
    )
    out_specs = (
        P("seq", "head"),
        P("seq", "head"),
        P("seq", "head"),
        P("seq", "head"),
        P("head", None),
    )
    return jax.shard_map(local, mesh=mesh, in_specs=in_specs, out_specs=out_specs, check_vma=False)
```

profile of v0, /device:TPU:1, one launch (start us, length us, event | category | flops | bytes accessed | tf_op | source)
XLA Modules:
  0.0 636.8 jit_solution(5743290585087357606)
XLA Ops:
  8.0 6.7 %select_convert_fusion.2 = bf16[768,512]{1,0:T(8,128)(2,1)} fusion(bf16[768,512]{1,0:T(8,128)(2,1)} %param.14, s32[768]{0:T(1024)S(1)} %get-tuple-element.251, s32[512]{0:T(512)S(1)} %get-tuple-element.253, s32[]{:T(128)} %bitcast.69, s32[512]{0:T(512)S(1)} %get-tuple-element.254, s32[768]{0:T(1024)S(1)} %get-tuple-element.252), kind=kLoop, calls=%fused_computation.25 | loop fusion | flops 14548992 | bytes 1583108 | tf_op jit(solution)/shard_map/convert_element_type | solution.py:90
  14.8 1.8 reshape.96
  16.6 2.4 reshape.97
  19.0 3.1 fusion.47
  22.2 2.4 reshape.98
  24.7 1.9 fusion.21
  26.6 2.9 select_convert_fusion.1
  29.4 31.4 %all-gather.6.cloned.1.call-done = bf16[768,2048]{1,0:T(8,128)(2,1)} async-done(((bf16[768,512]{1,0:T(8,128)(2,1)}), bf16[768,2048]{1,0:T(8,128)(2,1)}) %all-gather.6.cloned.1.call-update) | async-done | bytes 3145744 | tf_op jit(solution)/shard_map/all_gather | solution.py:91
  60.8 4.9 fusion.50
  65.7 2.8 reshape.100
  68.4 2.6 copy.66
  71.0 76.3 %all-gather.8.cloned.1.call-done = bf16[256,128,128]{2,1,0:T(8,128)(2,1)} async-done(((bf16[4,128,128]{2,1,0:T(8,128)(2,1)}), bf16[256,128,128]{2,1,0:T(8,128)(2,1)}) %all-gather.8.cloned.1.call-update) | async-done | bytes 8388624 | tf_op jit(solution)/shard_map/all_gather | solution.py:18
  147.2 67.8 %while.30 = (s32[]{:T(128)}, f32[4,128,128]{2,1,0:T(8,128)S(1)}, s32[]{:T(128)}, bf16[64,4,128,128]{3,2,1,0:T(8,128)(2,1)}, s32[]{:T(128)}, /*index=5*/s32[]{:T(128)}) while((s32[]{:T(128)}, f32[4,128,128]{2,1,0:T(8,128)S(1)}, s32[]{:T(128)}, bf16[64,4,128,128]{3,2,1,0:T(8,128)(2,1)}, s32[]{:T(128)}, /*index=5*/s32[]{:T(128)}) %tuple.95), condition=%wide.region_2.3_spmd.clone, body=%wide.region_1.2_spmd.clone.sunk | while | flops 262148 | bytes 655453 | solution.py:27
  149.4 1.0 add_select_fusion.8
  150.4 1.0 add_select_fusion.8
  152.5 1.0 add_select_fusion.8
  153.6 1.0 add_select_fusion.8
  154.7 1.0 add_select_fusion.8
  155.7 1.0 add_select_fusion.8
  156.8 1.0 add_select_fusion.8
  157.8 1.0 add_select_fusion.8
  160.0 1.0 add_select_fusion.8
  161.0 1.0 add_select_fusion.8
  163.1 1.0 add_select_fusion.8
  164.2 1.0 add_select_fusion.8
  166.3 1.0 add_select_fusion.8
  167.4 1.0 add_select_fusion.8
  169.5 1.0 add_select_fusion.8
  170.6 1.0 add_select_fusion.8
  172.7 1.0 add_select_fusion.8
  173.7 1.0 add_select_fusion.8
  174.8 1.0 add_select_fusion.8
  175.9 1.0 add_select_fusion.8
  176.9 1.0 add_select_fusion.8
  178.0 1.0 add_select_fusion.8
  180.1 1.0 add_select_fusion.8
  181.2 1.0 add_select_fusion.8
  215.1 1.9 fusion.31
  217.1 2.2 multiply_reduce_fusion
  219.3 1.6 multiply_convert_fusion.1
  220.9 2.2 copy.64
  223.0 5.9 fusion.16
  229.0 4.6 convolution_convert_fusion
  235.0 1.2 fusion.48
  237.0 1.1 slice.9
  238.9 1.1 fusion.49
  240.9 1.5 fusion.38
  243.0 1.2 copy-done.10
  244.2 1.6 fusion.8
  245.8 2.2 copy.72
  248.0 2.3 copy.140
  250.2 1.5 fusion.51
  251.8 168.5 %all-reduce.4.cloned.1.call-done = f32[512,2048]{1,0:T(8,128)} async-done(((f32[512,2048]{1,0:T(8,128)}), f32[512,2048]{1,0:T(8,128)}) %all-reduce.4.cloned.1.call-update) | async-done | bytes 4194320 | tf_op jit(solution)/shard_map/psum | solution.py:101
  420.3 4.0 multiply_convert_fusion
  424.3 39.8 %reduce-scatter.2.cloned.1.call-done = bf16[768,512]{1,0:T(8,128)(2,1)} async-done(((bf16[768,2048]{1,0:T(8,128)(2,1)}), bf16[768,512]{1,0:T(8,128)(2,1)}) %reduce-scatter.2.cloned.1.call-update) | async-done | bytes 786448 | tf_op jit(solution)/shard_map/reduce_scatter | solution.py:82
  464.1 6.7 %select_convert_fusion.3 = bf16[768,512]{1,0:T(8,128)(2,1)} fusion(bf16[768,512]{1,0:T(8,128)(2,1)} %reduce-scatter.2.cloned.1.call-done, s32[768]{0:T(1024)S(1)} %get-tuple-element.251, s32[512]{0:T(512)S(1)} %get-tuple-element.253, s32[]{:T(128)} %bitcast.68, s32[512]{0:T(512)S(1)} %get-tuple-element.254, s32[768]{0:T(1024)S(1)} %get-tuple-element.252), kind=kLoop, calls=%fused_computation.26 | loop fusion | flops 14548992 | bytes 1583108 | tf_op jit(solution)/shard_map/convert_element_type | solution.py:89
  470.8 79.4 %all-gather.10.cloned.1.call-done = bf16[256,128,128]{2,1,0:T(8,128)(2,1)} async-done(((bf16[4,128,128]{2,1,0:T(8,128)(2,1)}), bf16[256,128,128]{2,1,0:T(8,128)(2,1)}) %all-gather.10.cloned.1.call-update) | async-done | bytes 8388624 | tf_op jit(solution)/shard_map/all_gather | solution.py:18
  550.2 68.3 %while.31 = (s32[]{:T(128)}, f32[4,128,128]{2,1,0:T(8,128)S(1)}, s32[]{:T(128)}, bf16[64,4,128,128]{3,2,1,0:T(8,128)(2,1)}, s32[]{:T(128)}, /*index=5*/s32[]{:T(128)}, s32[]{:T(128)}, s32[]{:T(128)}) while((s32[]{:T(128)}, f32[4,128,128]{2,1,0:T(8,128)S(1)}, s32[]{:T(128)}, bf16[64,4,128,128]{3,2,1,0:T(8,128)(2,1)}, s32[]{:T(128)}, ...), condition=%wide.region_9.10_spmd.clone, body=%wide.region_8.9_spmd.clone.sunk | while | flops 262152 | bytes 655515 | solution.py:27
  550.2 1.1 add_select_fusion.9
  618.7 1.6 fusion.34
  620.3 1.3 fusion.15
  621.5 1.6 copy.83
  624.8 2.9 fusion.7
  627.7 1.5 copy.81
  (152 shorter events, 114.6 us)
Async XLA Ops:
  7.2 53.6 %copy-start = (bf16[512,2048]{1,0:T(8,128)(2,1)S(1)}, bf16[512,2048]{1,0:T(8,128)(2,1)}, u32[]{:S(2)}) copy-start(bf16[512,2048]{1,0:T(8,128)(2,1)} %param.13) | copy-start | bytes 6291460
  7.2 53.6 %all-gather.6.cloned.1.call-start = ((), (), s32[]{:S(2)}) async-start(), calls=%async_computation.2 | async-start | bytes 3932160 | tf_op jit(solution)/shard_map/all_gather | solution.py:91
  14.8 132.5 %all-gather.8.cloned.1.call-start = ((), (), s32[]{:S(2)}) async-start(), calls=%async_computation.4 | async-start | bytes 8519680 | tf_op jit(solution)/shard_map/all_gather | solution.py:18
  22.2 398.1 %all-reduce.4.cloned.1.call-start = ((), (), s32[]{:S(2)}) async-start(), calls=%async_computation.3 | async-start | bytes 8388608 | tf_op jit(solution)/shard_map/psum | solution.py:101
  215.1 1.9 copy-start.2
  215.1 2.0 copy-start.6
  229.0 235.1 %reduce-scatter.2.cloned.1.call-start = ((), (), s32[]{:S(2)}) async-start(), calls=%async_computation.1 | async-start | bytes 3932160 | tf_op jit(solution)/shard_map/reduce_scatter | solution.py:82
  233.6 1.1 copy-start.3
  233.6 1.4 copy-start.5
  233.6 316.6 %all-gather.10.cloned.1.call-start = ((), (), s32[]{:S(2)}) async-start(), calls=%async_computation.5 | async-start | bytes 8519680 | tf_op jit(solution)/shard_map/all_gather | solution.py:18
  240.9 1.5 copy-start.7
  243.0 1.2 copy-start.10
  247.9 2.3 copy-start.9
  550.2 68.5 %copy-start.12 = (f32[2,4,128,128]{2,3,1,0:T(8,128)S(1)}, f32[2,4,128,128]{2,3,1,0:T(8,128)}, u32[]{:S(2)}) copy-start(f32[2,4,128,128]{2,3,1,0:T(8,128)} %rev.8) | copy-start | bytes 1572868
  618.7 1.6 copy-start.11
  621.5 2.6 copy-start.4
  623.1 1.7 copy-start.8
  624.8 5.4 copy-start.1
Sparse Core Ops, SparseCore 0:
  14.9 45.8 all-gather.5
  63.6 83.6 all-gather.7
  229.1 191.1 all-reduce.3
  422.8 41.1 reduce-scatter.1
  467.1 83.0 all-gather.9
where the time goes:
time: 640 us; the launch traced here: 637 us
  waiting for transfers between devices  395 us (62%)
  other arithmetic  155 us (24%)
  matrix products  37.6 us (6%)
  local copies, waits for them, and re-layouts  30.5 us (5%)
  between operations  14.8 us (2%)
    psum x1, waiting for transfers between devices, local(): summed = lax.psum(weight_term, 'seq')  169 us
    all_gather x2, waiting for transfers between devices, prefix(): everything = lax.all_gather(value.astype(jnp.bfloat16), axis)  156 us
    select_n x128, other arithmetic, hop(): return jnp.where(reached, new, before)  133 us
    reduce_scatter x1, waiting for transfers between devices, local(): lax.psum_scatter(partial_value.astype(jnp.bfloat16), 'head', scatter_dime...  39.8 us
    all_gather x1, waiting for transfers between devices, local(): piece = lax.all_gather(grad_proj, 'head', axis=1, tiled=True)  31.4 us
  transfers between devices with their start and end apart: 5, of which 5 were waited for; matrix products, arithmetic and copies ran while one was open for 9% of the time, Pallas kernels for 0%

commit v1 on v0

v1 whole, which is shorter than its diff:
```python
import functools
import math

import jax
import jax.numpy as jnp
import numpy as np
from jax import lax
from jax.experimental import pallas as pl
from jax.experimental.pallas import tpu as pltpu
from jax.sharding import PartitionSpec as P

HD = 128
SPAN = 256
ROWS = 768
WIDTH = 512
MODEL = 2048
BLOCKS = ROWS // SPAN
HEADS = WIDTH // HD
N_ROW = 8
N_Z = 8
N_X = 4
HALF = SPAN // 2
EPS = 1e-05
KEEP_SCALE = 1.0 / 0.9
MODULUS = 32749.0
INVERSE = float(np.float32((1.0 - 2.0**-22) / 32749.0))
GRAD_SCALE = 1.0 / math.sqrt(49152)
MESH = pl.DeviceIdType.MESH
F32 = jnp.float32
BF16 = jnp.bfloat16

NN = (((1,), (0,)), ((), ()))
NT = (((1,), (1,)), ((), ()))
TN = (((0,), (0,)), ((), ()))


def dot(a, b, dims=NN):
    return lax.dot_general(a, b, dims, preferred_element_type=F32)


def wrap(value):
    quotient = jnp.floor(value * INVERSE)
    rest = value - quotient * MODULUS
    return jnp.where(rest >= MODULUS, rest - MODULUS, rest)


def keep_scales(positions, features, seed):
    mixing = wrap((positions * 181 + seed).astype(F32) + (features * 227).astype(F32))
    whole = mixing.astype(jnp.int32)
    square = whole * whole
    quotient = jnp.floor(square.astype(F32) * INVERSE).astype(jnp.int32)
    rest = square - quotient * 32749
    rest = jnp.where(rest >= 32749, rest - 32749, rest).astype(F32)
    offsets = (positions * 7).astype(F32) + (features * 13).astype(F32)
    hashed = wrap(rest * 173.0 + mixing * 59.0 + offsets)
    tens = jnp.floor((hashed + 0.5) * 0.1)
    return jnp.where(hashed - tens * 10.0 != 0.0, KEEP_SCALE, 0.0).astype(F32)


def rows(block):
    return pl.ds(block * SPAN, SPAN)


def half_rows(block, half):
    return pl.ds(block * SPAN + half * HALF, HALF)


def head(h):
    return pl.ds(h * HD, HD)


def kernel(
    seed_ref, q_hbm, k_hbm, v_hbm, w_hbm, go_hbm,
    out_hbm, gq_hbm, gk_hbm, gv_hbm, gw_hbm,
    q, k, v, go, w, scale, gp, kv, cs, state, mixed, inv, normed, turned,
    ps, own, relay_in, rin, gn, gm, gkv, gk_acc, gv_acc, out_b, gq_b, gk_b, gv_b,
    f_sb, f_rb, f_zs, f_zb, f_pb, f_fb, b_sb, b_rb, b_zs, b_zb, b_pb, b_fb,
    wsend, wown, wrecv, xs, xb, zsw, zbw, zone, zg, xg, pg,
    load_sem, store_sem, ag_s, ag_r, agr_s, agr_r, rs_s, rs_r,
    scan_s, scan_r, core_s, core_r, wx_s, wx_r, wz_s, wz_r,
):
    seq = lax.axis_index("seq")
    y = lax.axis_index("head")
    z = seq // N_ROW
    r = seq % N_ROW
    x = r // 2
    c = r % 2
    other = 1 - c

    def at(zz, rr, yy):
        return {"seq": zz * N_ROW + rr, "head": yy}

    y_next, y_prev, y_far = (y + 1) % 4, (y + 3) % 4, (y + 2) % 4
    beside = (at(z, r, y_next), at(z, r, y_prev))
    partner = at(z, x * 2 + other, y)

    def row_peer(i):
        return (r + i) % N_ROW

    def z_peer(i):
        return (z + i) % N_Z

    def x_peer(i):
        return (x + i) % N_X

    def remote(src, dst, send, recv, device):
        return pltpu.make_async_remote_copy(
            src_ref=src, dst_ref=dst, send_sem=send, recv_sem=recv,
            device_id=device, device_id_type=MESH,
        )

    loads = [
        pltpu.make_async_copy(a, b, load_sem.at[i])
        for i, (a, b) in enumerate(
            ((go_hbm, go), (k_hbm, k), (v_hbm, v), (q_hbm, q), (w_hbm, w))
        )
    ]
    for load in loads:
        load.start()

    barrier = pltpu.get_barrier_semaphore()
    for device in beside:
        pl.semaphore_signal(barrier, inc=1, device_id=device, device_id_type=MESH)

    def greet(i, _):
        pl.semaphore_signal(
            barrier, inc=1, device_id=at(z, row_peer(i), y), device_id_type=MESH
        )
        pl.semaphore_signal(
            barrier, inc=1, device_id=at(z_peer(i), r, y), device_id_type=MESH
        )
        return 0

    lax.fori_loop(1, N_ROW, greet, 0)

    def ag_own(b, way):
        return remote(
            gp.at[0, rows(b)], gp.at[1 + way, rows(b)], ag_s.at[way, b], ag_r.at[way, b],
            beside[way],
        )

    def ag_relay(b, way):
        part = half_rows(b, way)
        return remote(
            gp.at[1 + way, part], gp.at[3, part], agr_s.at[way, b], agr_r.at[way, b],
            beside[way],
        )

    seed = seed_ref[0]
    first_row = seq * ROWS
    first_column = y * WIDTH
    features = first_column + lax.broadcasted_iota(jnp.int32, (1, WIDTH), 1)
    TILE = 16

    def mask(b):
        def step(i, _):
            start = pl.multiple_of(b * SPAN + i * TILE, TILE)
            positions = first_row + start + lax.broadcasted_iota(jnp.int32, (TILE, 1), 0)
            kept = keep_scales(positions, features, seed)
            at_rows = pl.ds(start, TILE)
            scale[at_rows, :] = kept
            gp[0, at_rows, :] = (go[at_rows, :].astype(F32) * kept).astype(BF16)
            return 0

        lax.fori_loop(0, SPAN // TILE, step, 0)

    loads[0].wait()
    mask(0)
    loads[1].wait()
    loads[2].wait()

    def block_states(b, _):
        at_rows = pl.ds(pl.multiple_of(b * SPAN, SPAN), SPAN)
        for h in range(HEADS):
            kv[b, h] = dot(k[at_rows, head(h)], v[at_rows, head(h)], TN)
        return 0

    lax.fori_loop(0, BLOCKS, block_states, 0)

    def fill(sb, parts):
        for h in range(HEADS):
            total = (parts[0, h] + parts[1, h] + parts[2, h]).astype(BF16)
            sb[2 * h] = total[: HD // 2]
            sb[2 * h + 1] = total[HD // 2 :]

    def scan_one(n, i, sb, rb):
        t = row_peer(i)
        return remote(sb.at[t], rb.at[r], scan_s.at[n, 0, i], scan_r.at[n, 0, i], at(z, t, y))

    def scan_two(n, i, zs, zb):
        t = z_peer(i)
        return remote(zs, zb.at[z], scan_s.at[n, 1, i], scan_r.at[n, 1, i], at(t, r, y))

    def scan_three(n, i, pb, fb):
        t = row_peer(i)
        return remote(pb.at[t], fb.at[r], scan_s.at[n, 2, i], scan_r.at[n, 2, i], at(z, t, y))

    def loop(count, act):
        def step(i, _):
            act(i)
            return 0

        lax.fori_loop(1, count, step, 0)

    def row_from(i):
        return (r + N_ROW - i) % N_ROW

    def z_from(i):
        return (z + N_Z - i) % N_Z

    def x_from(i):
        return (x + N_X - i) % N_X

    def scan_start(n, sb, rb):
        rb[r] = sb[r]
        loop(N_ROW, lambda i: scan_one(n, i, sb, rb).start())

    def scan_middle(n, rb, zs, zb):
        loop(
            N_ROW,
            lambda i: remote(
                rb.at[0], rb.at[row_from(i)], scan_s.at[n, 0, i], scan_r.at[n, 0, i], partner
            ).wait_recv(),
        )
        total = rb[0].astype(F32)
        for j in range(1, N_ROW):
            total = total + rb[j].astype(F32)
        total = total.astype(BF16)
        zs[...] = total
        zb[z] = total
        loop(N_Z, lambda i: scan_two(n, i, zs, zb).start())

    def scan_late(n, rb, zb, pb, fb, reverse):
        loop(
            N_Z,
            lambda i: remote(
                zb.at[0], zb.at[z_from(i)], scan_s.at[n, 1, i], scan_r.at[n, 1, i], partner
            ).wait_recv(),
        )
        run = jnp.zeros((HD // 2, HD), F32)
        for j in range(N_Z):
            wanted = (j > z) if reverse else (j < z)
            run = run + jnp.where(wanted, zb[j].astype(F32), 0.0)
        order = range(N_ROW - 1, -1, -1) if reverse else range(N_ROW)
        for j in order:
            pb[j] = run.astype(BF16)
            run = run + rb[j].astype(F32)
        fb[r] = pb[r]
        loop(N_ROW, lambda i: scan_three(n, i, pb, fb).start())

    def scan_end(n, fb):
        loop(
            N_ROW,
            lambda i: remote(
                fb.at[0], fb.at[row_from(i)], scan_s.at[n, 2, i], scan_r.at[n, 2, i], partner
            ).wait_recv(),
        )

    def scan_sent(n, sb, rb, zs, zb, pb, fb):
        loop(N_ROW, lambda i: scan_one(n, i, sb, rb).wait_send())
        loop(N_Z, lambda i: scan_two(n, i, zs, zb).wait_send())
        loop(N_ROW, lambda i: scan_three(n, i, pb, fb).wait_send())

    fill(f_sb, kv)
    pl.semaphore_wait(barrier, 2 + N_ROW - 1 + N_Z - 1)
    scan_start(0, f_sb, f_rb)
    for way in range(2):
        ag_own(0, way).start()
    for b in range(1, BLOCKS):
        mask(b)
        for way in range(2):
            ag_own(b, way).start()
    scan_middle(0, f_rb, f_zs, f_zb)

    loads[3].wait()
    causal = lax.broadcasted_iota(jnp.int32, (SPAN, SPAN), 0) >= lax.broadcasted_iota(
        jnp.int32, (SPAN, SPAN), 1
    )

    def scores(b, _):
        at_rows = pl.ds(pl.multiple_of(b * SPAN, SPAN), SPAN)
        for h in range(HEADS):
            value = dot(q[at_rows, head(h)], k[at_rows, head(h)], NT)
            value = jnp.where(causal, value, 0.0).astype(BF16)
            cs[b * HEADS + h] = value
            mixed[at_rows, head(h)] = dot(value, v[at_rows, head(h)])
        return 0

    lax.fori_loop(0, BLOCKS, scores, 0)
    scan_late(0, f_rb, f_zb, f_pb, f_fb, False)
    loads[4].wait()

    def columns(block):
        return pl.ds(pl.multiple_of(block * WIDTH, WIDTH), WIDTH)

    model_block = (y, y_prev, y_next, y_far)

    def grad_normed(slot, b):
        def go_on(b, _):
            at_rows = pl.ds(pl.multiple_of(b * SPAN, SPAN), SPAN)
            term = dot(gp[slot, at_rows, :], w[:, columns(model_block[slot])], NT)
            gn[at_rows, :] = term if slot == 0 else gn[at_rows, :] + term
            return 0

        lax.fori_loop(b, b + 1, go_on, 0) if b is not None else lax.fori_loop(
            0, BLOCKS, go_on, 0
        )

    grad_normed(0, None)
    for way in range(2):
        ag_own(0, way).wait_recv()
        ag_relay(0, way).start()
    scan_end(0, f_fb)

    def mix(b, _):
        at_rows = pl.ds(pl.multiple_of(b * SPAN, SPAN), SPAN)
        for h in range(HEADS):
            run = jnp.concatenate([f_fb[2 * h], f_fb[2 * h + 1]], axis=0).astype(F32)
            for earlier in range(BLOCKS - 1):
                run = run + jnp.where(earlier < b, kv[earlier, h], 0.0)
            held = run.astype(BF16)
            state[b * HEADS + h] = held
            value = mixed[at_rows, head(h)] + dot(q[at_rows, head(h)], held)
            mixed[at_rows, head(h)] = value
            power = jnp.sum(value * value, axis=1, keepdims=True) * (1.0 / HD)
            inverse = lax.rsqrt(power + EPS)
            inv[at_rows, head(h)] = jnp.broadcast_to(inverse, (SPAN, HD))
            normed[at_rows, head(h)] = (value * inverse).astype(BF16)
        turned[:, at_rows] = normed[at_rows, :].T
        return 0

    lax.fori_loop(0, BLOCKS, mix, 0)

    def rs_first(b, way):
        return remote(
            ps.at[2, half_rows(b, way)], relay_in.at[way, b],
            rs_s.at[way, 0, b], rs_r.at[way, 0, b], beside[way],
        )

    def rs_plain(b, way):
        part = half_rows(b, 1 - way)
        return remote(
            ps.at[way, part], rin.at[way, part], rs_s.at[way, 1, b], rs_r.at[way, 1, b],
            beside[way],
        )

    def rs_added(b, way):
        part = half_rows(b, way)
        return remote(
            ps.at[way, part], rin.at[way, part], rs_s.at[way, 2, b], rs_r.at[way, 2, b],
            beside[way],
        )

    for way in range(2):
        ag_own(1, way).wait_recv()
        ag_relay(1, way).start()
    for slot, block in ((2, y_far), (0, y_next), (1, y_prev)):
        for b in range(BLOCKS):
            ps[slot, rows(b), :] = dot(normed[rows(b), :], w[:, columns(block)]).astype(BF16)
            if slot == 2:
                for way in range(2):
                    rs_first(b, way).start()
            else:
                rs_plain(b, slot).start()

    half = WIDTH // 2

    def core_out(j):
        return remote(wsend.at[j], wrecv.at[j], core_s.at[0, j], core_r.at[0, j], partner)

    def core_back(j):
        return remote(xg.at[j], pg.at[j], core_s.at[1, j], core_r.at[1, j], partner)

    def x_out(j, i):
        t = x_peer(i)
        return remote(
            xs.at[j, t], xb.at[j, x], wx_s.at[0, j, i], wx_r.at[0, j, i], at(z, t * 2 + c, y)
        )

    def x_back(j, i):
        t = x_peer(i)
        return remote(
            xg.at[j, x], xg.at[j, x], wx_s.at[1, j, i], wx_r.at[1, j, i], at(z, t * 2 + c, y)
        )

    def z_out(j, i):
        t = z_peer(i)
        return remote(
            zsw.at[j, t], zbw.at[j, z], wz_s.at[0, j, i], wz_r.at[0, j, i], at(t, r, y)
        )

    def z_back(j, i):
        t = z_peer(i)
        return remote(zone.at[j], zg.at[j, z], wz_s.at[1, j, i], wz_r.at[1, j, i], at(t, r, y))

    def w_start(j):
        theirs = pl.ds(pl.multiple_of(other * half, half), half)
        wsend[j] = dot(turned[theirs, :], gp[j]).astype(BF16)
        core_out(j).start()
        mine = pl.ds(pl.multiple_of(c * half, half), half)
        wown[j] = dot(turned[mine, :], gp[j])

    def w_x(j):
        core_out(j).wait_recv()
        for t in range(N_X):
            part = pl.ds(t * 64, 64)
            xs[j, t] = (wown[j, part, :] + wrecv[j, part, :].astype(F32)).astype(BF16)
        xb[j, x] = xs[j, x]
        loop(N_X, lambda i: x_out(j, i).start())

    def w_z(j):
        loop(
            N_X,
            lambda i: remote(
                xs.at[j, 0], xb.at[j, x_from(i)], wx_s.at[0, j, i], wx_r.at[0, j, i], partner
            ).wait_recv(),
        )
        total = xb[j, 0].astype(F32)
        for t in range(1, N_X):
            total = total + xb[j, t].astype(F32)
        total = total.astype(BF16)
        for t in range(N_Z):
            zsw[j, t] = total[(t // 2) * 16 : (t // 2) * 16 + 16, (t % 2) * 256 : (t % 2) * 256 + 256]
        zbw[j, z] = zsw[j, z]
        loop(N_Z, lambda i: z_out(j, i).start())

    def w_turn(j):
        loop(
            N_Z,
            lambda i: remote(
                zsw.at[j, 0], zbw.at[j, z_from(i)], wz_s.at[0, j, i], wz_r.at[0, j, i], partner
            ).wait_recv(),
        )
        total = zbw[j, 0].astype(F32)
        for t in range(1, N_Z):
            total = total + zbw[j, t].astype(F32)
        total = (total * GRAD_SCALE).astype(BF16)
        zone[j] = total
        zg[j, z] = total
        loop(N_Z, lambda i: z_back(j, i).start())

    def w_x_back(j):
        loop(
            N_Z,
            lambda i: remote(
                zone.at[j], zg.at[j, z_from(i)], wz_s.at[1, j, i], wz_r.at[1, j, i], partner
            ).wait_recv(),
        )
        pieces = [
            jnp.concatenate([zg[j, 2 * t], zg[j, 2 * t + 1]], axis=1) for t in range(N_Z // 2)
        ]
        xg[j, x] = jnp.concatenate(pieces, axis=0)
        loop(N_X, lambda i: x_back(j, i).start())

    def w_store(j, own_half):
        source = xg.at[j] if own_half else pg.at[j]
        start = (c if own_half else other) * N_X
        return pltpu.make_async_copy(
            source,
            gw_hbm.at[pl.ds(start, N_X), :, columns(model_block[j])],
            store_sem.at[4 + 2 * j + (0 if own_half else 1)],
        )

    def w_core_back(j):
        loop(
            N_X,
            lambda i: remote(
                xg.at[j, 0], xg.at[j, x_from(i)], wx_s.at[1, j, i], wx_r.at[1, j, i], partner
            ).wait_recv(),
        )
        core_back(j).start()
        w_store(j, True).start()

    def w_end(j):
        core_back(j).wait_recv()
        w_store(j, False).start()

    def w_sent(j):
        core_out(j).wait_send()
        core_back(j).wait_send()
        loop(N_X, lambda i: x_out(j, i).wait_send())
        loop(N_X, lambda i: x_back(j, i).wait_send())
        loop(N_Z, lambda i: z_out(j, i).wait_send())
        loop(N_Z, lambda i: z_back(j, i).wait_send())

    w_start(0)
    for way in range(2):
        ag_own(2, way).wait_recv()
        ag_relay(2, way).start()
    w_start(1)
    w_x(0)
    w_start(2)
    w_x(1)
    grad_normed(1, None)
    w_z(0)
    w_x(2)
    grad_normed(2, None)
    w_z(1)
    for b in range(BLOCKS):
        own[rows(b), :] = dot(normed[rows(b), :], w[:, columns(y)])
    w_turn(0)
    w_z(2)

    for b in range(BLOCKS):
        for way in range(2):
            ag_relay(b, way).wait_recv()

    w_start(3)
    grad_normed(3, None)

    def back_mix(b, _):
        at_rows = pl.ds(pl.multiple_of(b * SPAN, SPAN), SPAN)
        for h in range(HEADS):
            grad = gn[at_rows, head(h)]
            value = mixed[at_rows, head(h)]
            inverse = inv[at_rows, head(h)]
            mean = jnp.sum(grad * value, axis=1, keepdims=True) * (1.0 / HD)
            held = (inverse * (grad - value * inverse * inverse * mean)).astype(BF16)
            gm[at_rows, head(h)] = held
            gkv[b, h] = dot(q[at_rows, head(h)], held, TN)
        return 0

    lax.fori_loop(0, BLOCKS, back_mix, 0)
    fill(b_sb, gkv)
    scan_start(1, b_sb, b_rb)
    w_x(3)
    w_turn(1)
    w_x_back(0)

    def add_relayed(b):
        for way in range(2):
            rs_first(b, way).wait_recv()
            part = half_rows(b, way)
            both = ps[way, part, :].astype(F32) + relay_in[way, b].astype(F32)
            ps[way, part, :] = both.astype(BF16)
            rs_added(b, way).start()

    add_relayed(0)
    scan_middle(1, b_rb, b_zs, b_zb)
    w_z(3)
    add_relayed(1)
    w_turn(2)
    w_x_back(1)
    add_relayed(2)

    def back_local(b, _):
        at_rows = pl.ds(pl.multiple_of(b * SPAN, SPAN), SPAN)
        for h in range(HEADS):
            grad = gm[at_rows, head(h)]
            gs = dot(grad, v[at_rows, head(h)], NT)
            gs = jnp.where(causal, gs, 0.0).astype(BF16)
            gq_b[at_rows, head(h)] = (
                dot(grad, state[b * HEADS + h], NT) + dot(gs, k[at_rows, head(h)])
            ).astype(BF16)
            gk_acc[at_rows, head(h)] = dot(gs, q[at_rows, head(h)], TN)
            gv_acc[at_rows, head(h)] = dot(cs[b * HEADS + h], grad, TN)
        return 0

    lax.fori_loop(0, BLOCKS, back_local, 0)
    stores = [
        pltpu.make_async_copy(a, b, store_sem.at[i])
        for i, (a, b) in enumerate(
            ((gq_b, gq_hbm), (gk_b, gk_hbm), (gv_b, gv_hbm), (out_b, out_hbm))
        )
    ]
    stores[0].start()
    scan_late(1, b_rb, b_zb, b_pb, b_fb, True)
    w_core_back(0)
    w_turn(3)
    w_x_back(2)
    w_core_back(1)
    scan_end(1, b_fb)

    def back_end(b, _):
        at_rows = pl.ds(pl.multiple_of(b * SPAN, SPAN), SPAN)
        for h in range(HEADS):
            run = jnp.concatenate([b_fb[2 * h], b_fb[2 * h + 1]], axis=0).astype(F32)
            for later in range(1, BLOCKS):
                run = run + jnp.where(later > b, gkv[later, h], 0.0)
            held = run.astype(BF16)
            gk_b[at_rows, head(h)] = (
                gk_acc[at_rows, head(h)] + dot(v[at_rows, head(h)], held, NT)
            ).astype(BF16)
            gv_b[at_rows, head(h)] = (
                gv_acc[at_rows, head(h)] + dot(k[at_rows, head(h)], held)
            ).astype(BF16)
        return 0

    lax.fori_loop(0, BLOCKS, back_end, 0)
    stores[1].start()
    stores[2].start()
    w_x_back(3)
    w_core_back(2)
    w_end(0)
    w_end(1)
    w_core_back(3)
    w_end(2)

    for b in range(BLOCKS):
        for way in range(2):
            rs_plain(b, way).wait_recv()
    for b in range(BLOCKS):
        for way in range(2):
            rs_added(b, way).wait_recv()

        def finish(i, _):
            at_rows = pl.ds(pl.multiple_of(b * SPAN + i * 32, 32), 32)
            total = own[at_rows, :] + rin[0, at_rows, :].astype(F32) + rin[1, at_rows, :].astype(F32)
            out_b[at_rows, :] = (total * scale[at_rows, :]).astype(BF16)
            return 0

        lax.fori_loop(0, SPAN // 32, finish, 0)
    stores[3].start()
    w_end(3)

    for b in range(BLOCKS):
        for way in range(2):
            ag_own(b, way).wait_send()
            ag_relay(b, way).wait_send()
            rs_first(b, way).wait_send()
            rs_plain(b, way).wait_send()
            rs_added(b, way).wait_send()
    scan_sent(0, f_sb, f_rb, f_zs, f_zb, f_pb, f_fb)
    scan_sent(1, b_sb, b_rb, b_zs, b_zb, b_pb, b_fb)
    for j in range(4):
        w_sent(j)
        w_store(j, True).wait()
        w_store(j, False).wait()
    for store in stores:
        store.wait()


def local(queries, attn_keys, attn_values, out_weight, grad_out, drop_seed):
    square = (ROWS, WIDTH)
    vmem = pltpu.VMEM
    scan_buffers = [
        vmem((8, 64, 128), BF16),
        vmem((8, 64, 128), BF16),
        vmem((64, 128), BF16),
        vmem((8, 64, 128), BF16),
        vmem((8, 64, 128), BF16),
        vmem((8, 64, 128), BF16),
    ]
    dma = pltpu.SemaphoreType.DMA
    scratch = [
        vmem(square, BF16), vmem(square, BF16), vmem(square, BF16), vmem(square, BF16),
        vmem((WIDTH, MODEL), BF16),
        vmem(square, F32),
        vmem((4,) + square, BF16),
        vmem((BLOCKS, HEADS, HD, HD), F32),
        vmem((BLOCKS * HEADS, SPAN, SPAN), BF16),
        vmem((BLOCKS * HEADS, HD, HD), BF16),
        vmem(square, F32),
        vmem(square, F32),
        vmem(square, BF16),
        vmem((WIDTH, ROWS), BF16),
        vmem((3,) + square, BF16),
        vmem(square, F32),
        vmem((2, BLOCKS, HALF, WIDTH), BF16),
        vmem((2,) + square, BF16),
        vmem(square, F32),
        vmem(square, BF16),
        vmem((BLOCKS, HEADS, HD, HD), F32),
        vmem(square, F32), vmem(square, F32),
        vmem(square, BF16), vmem(square, BF16), vmem(square, BF16), vmem(square, BF16),
        *scan_buffers, *scan_buffers,
        vmem((4, 256, 512), BF16),
        vmem((4, 256, 512), F32),
        vmem((4, 256, 512), BF16),
        vmem((4, 4, 64, 512), BF16),
        vmem((4, 4, 64, 512), BF16),
        vmem((4, 8, 16, 256), BF16),
        vmem((4, 8, 16, 256), BF16),
        vmem((4, 16, 256), BF16),
        vmem((4, 8, 16, 256), BF16),
        vmem((4, 4, 64, 512), BF16),
        vmem((4, 4, 64, 512), BF16),
        dma((5,)), dma((12,)),
        dma((2, 3)), dma((2, 3)), dma((2, 3)), dma((2, 3)),
        dma((2, 3, 3)), dma((2, 3, 3)),
        dma((2, 3, 8)), dma((2, 3, 8)),
        dma((2, 4)), dma((2, 4)),
        dma((2, 4, 4)), dma((2, 4, 4)),
        dma((2, 4, 8)), dma((2, 4, 8)),
    ]
    hbm = pl.BlockSpec(memory_space=pl.ANY)
    outs = pl.pallas_call(
        kernel,
        out_shape=[jax.ShapeDtypeStruct(square, BF16)] * 4
        + [jax.ShapeDtypeStruct((8, 64, MODEL), BF16)],
        in_specs=[pl.BlockSpec(memory_space=pltpu.SMEM)] + [hbm] * 5,
        out_specs=[hbm] * 5,
        scratch_shapes=scratch,
        compiler_params=pltpu.CompilerParams(
            collective_id=0, has_side_effects=True, vmem_limit_bytes=60 * 1024 * 1024
        ),
        cost_estimate=pl.CostEstimate(
            flops=7_000_000_000, bytes_accessed=11_000_000, transcendentals=3072
        ),
        name="layer",
    )(drop_seed, queries, attn_keys, attn_values, out_weight, grad_out)
    output, grad_q, grad_k, grad_v, grad_w = outs
    return output, grad_q, grad_k, grad_v, grad_w.reshape(WIDTH, MODEL)


def solution(mesh):
    tokens = P("seq", "head")
    weight = P("head", None)
    return jax.shard_map(
        local,
        mesh=mesh,
        in_specs=(tokens, tokens, tokens, weight, tokens, P()),
        out_specs=(tokens, tokens, tokens, tokens, weight),
        check_vma=False,
    )
```

time: 640 us -> 95 us (0.15)
  waiting for transfers between devices: 395 us -> 0 us
  other arithmetic: 155 us -> 0 us
  Pallas kernels: 0 us -> 87.4 us
  matrix products: 37.6 us -> 0 us
  local copies, waits for them, and re-layouts: 30.5 us -> 6.19 us
  between operations: 14.8 us -> 1.32 us
    all_gather x3 -> x0, waiting for transfers between devices: 187 us -> none  [the longest x2 156 us: prefix(): everything = lax.all_gather(value.astype(jnp.bfloat16), axis)]
    psum x1 -> x0, waiting for transfers between devices: 169 us -> none  [local(): summed = lax.psum(weight_term, 'seq')]
    select_n x128 -> x0, other arithmetic: 133 us -> none  [hop(): return jnp.where(reached, new, before)]
    pallas_call x0 -> x1, Pallas kernels: none -> 87.4 us  [local(): pl.pallas_call(kernel, out_shape=[jax.ShapeDtypeStruct(square, BF16)] * 4...]
    reduce_scatter x1 -> x0, waiting for transfers between devices: 39.8 us -> none  [local(): lax.psum_scatter(partial_value.astype(jnp.bfloat16), 'head', scatter_dime...]
    dot_general x15 -> x0, matrix products: 37.6 us -> none  [the longest x1 5.93 us: local(): lax.dot_general(normed, piece, (((0,), (0,)), ((), ())), preferred_elemen...]
    convert_element_type x4 -> x0, other arithmetic: 19 us -> none  [the longest x1 6.69 us: local(): jnp.where(keep, grad_out.astype(jnp.float32) * keep_scale, 0.0)]
    reshape x5 -> x0, local copies, waits for them, and re-layouts: 12 us -> none  [the longest x3 6.64 us: split(): return array.reshape(n_blocks, SPAN, local_heads, HD)]
  transfers between devices with their start and end apart: 5 -> 0, of which waited for: 5 -> 0; matrix products, arithmetic and copies ran while one was open for 9% -> 0% of each run, Pallas kernels for 0% -> 0%
where the time goes in v1:
time: 95 us; the launch traced here: 94.9 us
  Pallas kernels  87.4 us (92%)
  local copies, waits for them, and re-layouts  6.19 us (7%)
  between operations  1.32 us (1%)
    pallas_call x1, Pallas kernels, local(): pl.pallas_call(kernel, out_shape=[jax.ShapeDtypeStruct(square, BF16)] * 4...  87.4 us
    unnamed x13, local copies, waits for them, and re-layouts  6.19 us

profile of v1, /device:TPU:1, one launch (start us, length us, event | category | flops | bytes accessed | tf_op | source)
XLA Modules:
  0.0 94.9 jit_solution(2072089162228760837)
XLA Ops:
  1.3 87.4 %layer.1 = (bf16[768,512]{1,0:T(8,128)(2,1)}, bf16[768,512]{1,0:T(8,128)(2,1)}, bf16[768,512]{1,0:T(8,128)(2,1)}, bf16[768,512]{1,0:T(8,128)(2,1)}, bf16[8,64,2048]{2,1,0:T(8,128)(2,1)}) custom-call(s32[1]{0:T(128)S(6)} %copy.16.seed_ref, bf16[768,512]{1,0:T(8,128)(2,1)} %q_hbm.1, bf16[768,512]{1,0:T(8,128)(2,1)} %k_hbm.1, bf16[768,512]{1,0:T(8,128)(2,1)} %v_hbm.1, ...), custom_call_target="tpu_custom_call" | custom-call | flops 7000000000 | bytes 11000000 | tf_op jit(solution)/shard_map/layer/pallas_call | solution.py:687
  88.7 0.0 copy-start.3
  88.7 0.0 copy-start.2
  88.7 0.0 copy-start.1
  88.7 2.2 %copy.17 = bf16[768,512]{1,0:T(8,128)(2,1)} copy(bf16[768,512]{1,0:T(8,128)(2,1)} %get-tuple-element.20) | data formatting | bytes 1572864
  90.9 0.0 copy-done.3
  90.9 0.0 copy-start
  90.9 0.9 copy.18
  91.8 0.0 copy-done.2
  91.8 0.9 copy.19
  92.7 0.0 copy-done.1
  92.7 0.9 copy.20
  93.6 0.0 copy-done
  93.6 1.3 %copy.21 = bf16[512,2048]{1,0:T(8,128)(2,1)} copy(bf16[512,2048]{1,0:T(8,128)(2,1)S(1)} %bitcast.1) | data formatting | bytes 4194304
Async XLA Ops:
  88.7 2.2 %copy-start.3 = (bf16[768,512]{1,0:T(8,128)(2,1)S(1)}, bf16[768,512]{1,0:T(8,128)(2,1)}, u32[]{:S(2)}) copy-start(bf16[768,512]{1,0:T(8,128)(2,1)} %get-tuple-element.21) | copy-start | bytes 2359300
  88.7 3.1 %copy-start.2 = (bf16[768,512]{1,0:T(8,128)(2,1)S(1)}, bf16[768,512]{1,0:T(8,128)(2,1)}, u32[]{:S(2)}) copy-start(bf16[768,512]{1,0:T(8,128)(2,1)} %get-tuple-element.22) | copy-start | bytes 2359300
  88.7 4.0 %copy-start.1 = (bf16[768,512]{1,0:T(8,128)(2,1)S(1)}, bf16[768,512]{1,0:T(8,128)(2,1)}, u32[]{:S(2)}) copy-start(bf16[768,512]{1,0:T(8,128)(2,1)} %get-tuple-element.23) | copy-start | bytes 2359300
  90.9 2.6 %copy-start = (bf16[8,64,2048]{2,1,0:T(8,128)(2,1)S(1)}, bf16[8,64,2048]{2,1,0:T(8,128)(2,1)}, u32[]{:S(2)}) copy-start(bf16[8,64,2048]{2,1,0:T(8,128)(2,1)} %get-tuple-element.14) | copy-start | bytes 6291460

commit v2 on v1

--- a/solution.py
+++ b/solution.py
@@ -34,6 +34,17 @@
 TN = (((0,), (0,)), ((), ()))
 
 
+ORDER = (
+    "go", "mask0", "states", "meet", "f1", "send0", "mask1", "send1", "mask2", "send2", "rest",
+    "f2", "scores", "f3", "weight", "gn0", "relay0", "relay1", "relay2", "f4", "mix",
+    "part_far", "w0_0", "part_next", "part_prev", "w1_0",
+    "own", "w2_0", "near", "w0_1", "w0_2", "gn1", "gn2", "w1_1", "w1_2",
+    "far", "gn3", "back_mix", "b1", "w0_3", "w3_0", "w1_3", "w2_1", "w2_2", "b2", "add0", "add1", "add2", "w2_3", "w4_0", "back_local",
+    "w3_1", "w3_2", "b3", "w3_3", "w5_0", "w4_1", "w4_2", "b4", "back_end", "w4_3", "w6_0", "w5_1", "w5_2",
+    "w5_3", "w6_1", "w6_2", "fin0", "fin1", "fin2", "w6_3",
+)
+
+
 def dot(a, b, dims=NN):
     return lax.dot_general(a, b, dims, preferred_element_type=F32)
 
@@ -71,12 +82,12 @@
 
 def kernel(
     seed_ref, q_hbm, k_hbm, v_hbm, w_hbm, go_hbm,
-    out_hbm, gq_hbm, gk_hbm, gv_hbm, gw_hbm,
+    out_b, gq_b, gk_b, gv_b, gw_out,
     q, k, v, go, w, scale, gp, kv, cs, state, mixed, inv, normed, turned,
-    ps, own, relay_in, rin, gn, gm, gkv, gk_acc, gv_acc, out_b, gq_b, gk_b, gv_b,
+    ps, own, relay_in, rin, gn, gm, gkv, gk_acc, gv_acc,
     f_sb, f_rb, f_zs, f_zb, f_pb, f_fb, b_sb, b_rb, b_zs, b_zb, b_pb, b_fb,
     wsend, wown, wrecv, xs, xb, zsw, zbw, zone, zg, xg, pg,
-    load_sem, store_sem, ag_s, ag_r, agr_s, agr_r, rs_s, rs_r,
+    load_sem, ag_s, ag_r, agr_s, agr_r, rs_s, rs_r,
     scan_s, scan_r, core_s, core_r, wx_s, wx_r, wz_s, wz_r,
 ):
     seq = lax.axis_index("seq")
@@ -109,6 +120,33 @@
             device_id=device, device_id_type=MESH,
         )
 
+    sent = []
+
+    def loop(count, act):
+        def step(i, _):
+            act(i)
+            return 0
+
+        lax.fori_loop(1, count, step, 0)
+
+    def start(copy):
+        copy.start()
+        sent.append(copy.wait_send)
+
+    def start_all(count, make):
+        loop(count, lambda i: make(i).start())
+        sent.append(lambda: loop(count, lambda i: make(i).wait_send()))
+
+    def put(copy):
+        copy.start()
+        sent.append(copy.wait)
+
+    def arrive(copy):
+        copy.wait_recv()
+
+    def arrive_all(count, make):
+        loop(count, lambda i: make(i).wait_recv())
+
     loads = [
         pltpu.make_async_copy(a, b, load_sem.at[i])
         for i, (a, b) in enumerate(
@@ -133,9 +171,10 @@
 
     lax.fori_loop(1, N_ROW, greet, 0)
 
-    def ag_own(b, way):
-        return remote(
-            gp.at[0, rows(b)], gp.at[1 + way, rows(b)], ag_s.at[way, b], ag_r.at[way, b],
+    def ag_own(b, way, late):
+        part = half_rows(b, 1 - way if late else way)
+        return remote(
+            gp.at[0, part], gp.at[1 + way, part], ag_s.at[way, late, b], ag_r.at[way, late, b],
             beside[way],
         )
 
@@ -164,19 +203,12 @@
 
         lax.fori_loop(0, SPAN // TILE, step, 0)
 
-    loads[0].wait()
-    mask(0)
-    loads[1].wait()
-    loads[2].wait()
-
     def block_states(b, _):
         at_rows = pl.ds(pl.multiple_of(b * SPAN, SPAN), SPAN)
         for h in range(HEADS):
             kv[b, h] = dot(k[at_rows, head(h)], v[at_rows, head(h)], TN)
         return 0
 
-    lax.fori_loop(0, BLOCKS, block_states, 0)
-
     def fill(sb, parts):
         for h in range(HEADS):
             total = (parts[0, h] + parts[1, h] + parts[2, h]).astype(BF16)
@@ -195,13 +227,6 @@
         t = row_peer(i)
         return remote(pb.at[t], fb.at[r], scan_s.at[n, 2, i], scan_r.at[n, 2, i], at(z, t, y))
 
-    def loop(count, act):
-        def step(i, _):
-            act(i)
-            return 0
-
-        lax.fori_loop(1, count, step, 0)
-
     def row_from(i):
         return (r + N_ROW - i) % N_ROW
 
@@ -213,30 +238,24 @@
 
     def scan_start(n, sb, rb):
         rb[r] = sb[r]
-        loop(N_ROW, lambda i: scan_one(n, i, sb, rb).start())
+        start_all(N_ROW, lambda i: scan_one(n, i, sb, rb))
 
     def scan_middle(n, rb, zs, zb):
-        loop(
-            N_ROW,
-            lambda i: remote(
+        arrive_all(N_ROW, lambda i: remote(
                 rb.at[0], rb.at[row_from(i)], scan_s.at[n, 0, i], scan_r.at[n, 0, i], partner
-            ).wait_recv(),
-        )
+            ))
         total = rb[0].astype(F32)
         for j in range(1, N_ROW):
             total = total + rb[j].astype(F32)
         total = total.astype(BF16)
         zs[...] = total
         zb[z] = total
-        loop(N_Z, lambda i: scan_two(n, i, zs, zb).start())
+        start_all(N_Z, lambda i: scan_two(n, i, zs, zb))
 
     def scan_late(n, rb, zb, pb, fb, reverse):
-        loop(
-            N_Z,
-            lambda i: remote(
+        arrive_all(N_Z, lambda i: remote(
                 zb.at[0], zb.at[z_from(i)], scan_s.at[n, 1, i], scan_r.at[n, 1, i], partner
-            ).wait_recv(),
-        )
+            ))
         run = jnp.zeros((HD // 2, HD), F32)
         for j in range(N_Z):
             wanted = (j > z) if reverse else (j < z)
@@ -246,33 +265,13 @@
             pb[j] = run.astype(BF16)
             run = run + rb[j].astype(F32)
         fb[r] = pb[r]
-        loop(N_ROW, lambda i: scan_three(n, i, pb, fb).start())
+        start_all(N_ROW, lambda i: scan_three(n, i, pb, fb))
 
     def scan_end(n, fb):
-        loop(
-            N_ROW,
-            lambda i: remote(
+        arrive_all(N_ROW, lambda i: remote(
                 fb.at[0], fb.at[row_from(i)], scan_s.at[n, 2, i], scan_r.at[n, 2, i], partner
-            ).wait_recv(),
-        )
-
-    def scan_sent(n, sb, rb, zs, zb, pb, fb):
-        loop(N_ROW, lambda i: scan_one(n, i, sb, rb).wait_send())
-        loop(N_Z, lambda i: scan_two(n, i, zs, zb).wait_send())
-        loop(N_ROW, lambda i: scan_three(n, i, pb, fb).wait_send())
-
-    fill(f_sb, kv)
-    pl.semaphore_wait(barrier, 2 + N_ROW - 1 + N_Z - 1)
-    scan_start(0, f_sb, f_rb)
-    for way in range(2):
-        ag_own(0, way).start()
-    for b in range(1, BLOCKS):
-        mask(b)
-        for way in range(2):
-            ag_own(b, way).start()
-    scan_middle(0, f_rb, f_zs, f_zb)
-
-    loads[3].wait()
+            ))
+
     causal = lax.broadcasted_iota(jnp.int32, (SPAN, SPAN), 0) >= lax.broadcasted_iota(
         jnp.int32, (SPAN, SPAN), 1
     )
@@ -286,31 +285,19 @@
             mixed[at_rows, head(h)] = dot(value, v[at_rows, head(h)])
         return 0
 
-    lax.fori_loop(0, BLOCKS, scores, 0)
-    scan_late(0, f_rb, f_zb, f_pb, f_fb, False)
-    loads[4].wait()
-
     def columns(block):
         return pl.ds(pl.multiple_of(block * WIDTH, WIDTH), WIDTH)
 
     model_block = (y, y_prev, y_next, y_far)
 
-    def grad_normed(slot, b):
+    def grad_normed(slot):
         def go_on(b, _):
             at_rows = pl.ds(pl.multiple_of(b * SPAN, SPAN), SPAN)
             term = dot(gp[slot, at_rows, :], w[:, columns(model_block[slot])], NT)
             gn[at_rows, :] = term if slot == 0 else gn[at_rows, :] + term
             return 0
 
-        lax.fori_loop(b, b + 1, go_on, 0) if b is not None else lax.fori_loop(
-            0, BLOCKS, go_on, 0
-        )
-
-    grad_normed(0, None)
-    for way in range(2):
-        ag_own(0, way).wait_recv()
-        ag_relay(0, way).start()
-    scan_end(0, f_fb)
+        lax.fori_loop(0, BLOCKS, go_on, 0)
 
     def mix(b, _):
         at_rows = pl.ds(pl.multiple_of(b * SPAN, SPAN), SPAN)
@@ -329,8 +316,6 @@
         turned[:, at_rows] = normed[at_rows, :].T
         return 0
 
-    lax.fori_loop(0, BLOCKS, mix, 0)
-
     def rs_first(b, way):
         return remote(
             ps.at[2, half_rows(b, way)], relay_in.at[way, b],
@@ -351,17 +336,14 @@
             beside[way],
         )
 
-    for way in range(2):
-        ag_own(1, way).wait_recv()
-        ag_relay(1, way).start()
-    for slot, block in ((2, y_far), (0, y_next), (1, y_prev)):
+    def partial(slot, block):
         for b in range(BLOCKS):
             ps[slot, rows(b), :] = dot(normed[rows(b), :], w[:, columns(block)]).astype(BF16)
             if slot == 2:
                 for way in range(2):
-                    rs_first(b, way).start()
+                    start(rs_first(b, way))
             else:
-                rs_plain(b, slot).start()
+                start(rs_plain(b, slot))
 
     half = WIDTH // 2
 
@@ -396,25 +378,22 @@
     def w_start(j):
         theirs = pl.ds(pl.multiple_of(other * half, half), half)
         wsend[j] = dot(turned[theirs, :], gp[j]).astype(BF16)
-        core_out(j).start()
+        start(core_out(j))
         mine = pl.ds(pl.multiple_of(c * half, half), half)
         wown[j] = dot(turned[mine, :], gp[j])
 
     def w_x(j):
-        core_out(j).wait_recv()
+        arrive(core_out(j))
         for t in range(N_X):
             part = pl.ds(t * 64, 64)
             xs[j, t] = (wown[j, part, :] + wrecv[j, part, :].astype(F32)).astype(BF16)
         xb[j, x] = xs[j, x]
-        loop(N_X, lambda i: x_out(j, i).start())
+        start_all(N_X, lambda i: x_out(j, i))
 
     def w_z(j):
-        loop(
-            N_X,
-            lambda i: remote(
+        arrive_all(N_X, lambda i: remote(
                 xs.at[j, 0], xb.at[j, x_from(i)], wx_s.at[0, j, i], wx_r.at[0, j, i], partner
-            ).wait_recv(),
-        )
+            ))
         total = xb[j, 0].astype(F32)
         for t in range(1, N_X):
             total = total + xb[j, t].astype(F32)
@@ -422,91 +401,46 @@
         for t in range(N_Z):
             zsw[j, t] = total[(t // 2) * 16 : (t // 2) * 16 + 16, (t % 2) * 256 : (t % 2) * 256 + 256]
         zbw[j, z] = zsw[j, z]
-        loop(N_Z, lambda i: z_out(j, i).start())
+        start_all(N_Z, lambda i: z_out(j, i))
 
     def w_turn(j):
-        loop(
-            N_Z,
-            lambda i: remote(
+        arrive_all(N_Z, lambda i: remote(
                 zsw.at[j, 0], zbw.at[j, z_from(i)], wz_s.at[0, j, i], wz_r.at[0, j, i], partner
-            ).wait_recv(),
-        )
+            ))
         total = zbw[j, 0].astype(F32)
         for t in range(1, N_Z):
             total = total + zbw[j, t].astype(F32)
         total = (total * GRAD_SCALE).astype(BF16)
         zone[j] = total
         zg[j, z] = total
-        loop(N_Z, lambda i: z_back(j, i).start())
+        start_all(N_Z, lambda i: z_back(j, i))
 
     def w_x_back(j):
-        loop(
-            N_Z,
-            lambda i: remote(
+        arrive_all(N_Z, lambda i: remote(
                 zone.at[j], zg.at[j, z_from(i)], wz_s.at[1, j, i], wz_r.at[1, j, i], partner
-            ).wait_recv(),
-        )
+            ))
         pieces = [
             jnp.concatenate([zg[j, 2 * t], zg[j, 2 * t + 1]], axis=1) for t in range(N_Z // 2)
         ]
         xg[j, x] = jnp.concatenate(pieces, axis=0)
-        loop(N_X, lambda i: x_back(j, i).start())
+        start_all(N_X, lambda i: x_back(j, i))
 
     def w_store(j, own_half):
-        source = xg.at[j] if own_half else pg.at[j]
-        start = (c if own_half else other) * N_X
-        return pltpu.make_async_copy(
-            source,
-            gw_hbm.at[pl.ds(start, N_X), :, columns(model_block[j])],
-            store_sem.at[4 + 2 * j + (0 if own_half else 1)],
-        )
+        source = xg if own_half else pg
+        first = (c if own_half else other) * N_X
+        for t in range(N_X):
+            gw_out[first + t, :, columns(model_block[j])] = source[j, t]
 
     def w_core_back(j):
-        loop(
-            N_X,
-            lambda i: remote(
+        arrive_all(N_X, lambda i: remote(
                 xg.at[j, 0], xg.at[j, x_from(i)], wx_s.at[1, j, i], wx_r.at[1, j, i], partner
-            ).wait_recv(),
-        )
-        core_back(j).start()
-        w_store(j, True).start()
+            ))
+        start(core_back(j))
+        w_store(j, True)
 
     def w_end(j):
-        core_back(j).wait_recv()
-        w_store(j, False).start()
-
-    def w_sent(j):
-        core_out(j).wait_send()
-        core_back(j).wait_send()
-        loop(N_X, lambda i: x_out(j, i).wait_send())
-        loop(N_X, lambda i: x_back(j, i).wait_send())
-        loop(N_Z, lambda i: z_out(j, i).wait_send())
-        loop(N_Z, lambda i: z_back(j, i).wait_send())
-
-    w_start(0)
-    for way in range(2):
-        ag_own(2, way).wait_recv()
-        ag_relay(2, way).start()
-    w_start(1)
-    w_x(0)
-    w_start(2)
-    w_x(1)
-    grad_normed(1, None)
-    w_z(0)
-    w_x(2)
-    grad_normed(2, None)
-    w_z(1)
-    for b in range(BLOCKS):
-        own[rows(b), :] = dot(normed[rows(b), :], w[:, columns(y)])
-    w_turn(0)
-    w_z(2)
-
-    for b in range(BLOCKS):
-        for way in range(2):
-            ag_relay(b, way).wait_recv()
-
-    w_start(3)
-    grad_normed(3, None)
+        arrive(core_back(j))
+        w_store(j, False)
 
     def back_mix(b, _):
         at_rows = pl.ds(pl.multiple_of(b * SPAN, SPAN), SPAN)
@@ -520,28 +454,13 @@
             gkv[b, h] = dot(q[at_rows, head(h)], held, TN)
         return 0
 
-    lax.fori_loop(0, BLOCKS, back_mix, 0)
-    fill(b_sb, gkv)
-    scan_start(1, b_sb, b_rb)
-    w_x(3)
-    w_turn(1)
-    w_x_back(0)
-
     def add_relayed(b):
         for way in range(2):
-            rs_first(b, way).wait_recv()
+            arrive(rs_first(b, way))
             part = half_rows(b, way)
             both = ps[way, part, :].astype(F32) + relay_in[way, b].astype(F32)
             ps[way, part, :] = both.astype(BF16)
-            rs_added(b, way).start()
-
-    add_relayed(0)
-    scan_middle(1, b_rb, b_zs, b_zb)
-    w_z(3)
-    add_relayed(1)
-    w_turn(2)
-    w_x_back(1)
-    add_relayed(2)
+            start(rs_added(b, way))
 
     def back_local(b, _):
         at_rows = pl.ds(pl.multiple_of(b * SPAN, SPAN), SPAN)
@@ -555,21 +474,6 @@
             gk_acc[at_rows, head(h)] = dot(gs, q[at_rows, head(h)], TN)
             gv_acc[at_rows, head(h)] = dot(cs[b * HEADS + h], grad, TN)
         return 0
-
-    lax.fori_loop(0, BLOCKS, back_local, 0)
-    stores = [
-        pltpu.make_async_copy(a, b, store_sem.at[i])
-        for i, (a, b) in enumerate(
-            ((gq_b, gq_hbm), (gk_b, gk_hbm), (gv_b, gv_hbm), (out_b, out_hbm))
-        )
-    ]
-    stores[0].start()
-    scan_late(1, b_rb, b_zb, b_pb, b_fb, True)
-    w_core_back(0)
-    w_turn(3)
-    w_x_back(2)
-    w_core_back(1)
-    scan_end(1, b_fb)
 
     def back_end(b, _):
         at_rows = pl.ds(pl.multiple_of(b * SPAN, SPAN), SPAN)
@@ -586,48 +490,122 @@
             ).astype(BF16)
         return 0
 
-    lax.fori_loop(0, BLOCKS, back_end, 0)
-    stores[1].start()
-    stores[2].start()
-    w_x_back(3)
-    w_core_back(2)
-    w_end(0)
-    w_end(1)
-    w_core_back(3)
-    w_end(2)
-
-    for b in range(BLOCKS):
+    def finish(b):
         for way in range(2):
-            rs_plain(b, way).wait_recv()
-    for b in range(BLOCKS):
-        for way in range(2):
-            rs_added(b, way).wait_recv()
-
-        def finish(i, _):
+            arrive(rs_plain(b, way))
+            arrive(rs_added(b, way))
+
+        def step(i, _):
             at_rows = pl.ds(pl.multiple_of(b * SPAN + i * 32, 32), 32)
             total = own[at_rows, :] + rin[0, at_rows, :].astype(F32) + rin[1, at_rows, :].astype(F32)
             out_b[at_rows, :] = (total * scale[at_rows, :]).astype(BF16)
             return 0
 
-        lax.fori_loop(0, SPAN // 32, finish, 0)
-    stores[3].start()
-    w_end(3)
-
+        lax.fori_loop(0, SPAN // 32, step, 0)
+
+    def blocks(body):
+        lax.fori_loop(0, BLOCKS, body, 0)
+
+    def do_send(b):
+        for way in range(2):
+            start(ag_own(b, way, 0))
+
+    def do_rest():
+        for b in range(BLOCKS):
+            for way in range(2):
+                start(ag_own(b, way, 1))
+
+    def do_relay(b):
+        for way in range(2):
+            arrive(ag_own(b, way, 0))
+            start(ag_relay(b, way))
+
+    def do_near():
+        for b in range(BLOCKS):
+            for way in range(2):
+                arrive(ag_own(b, way, 1))
+
+    def do_far():
+        for b in range(BLOCKS):
+            for way in range(2):
+                arrive(ag_relay(b, way))
+
+    def do_states():
+        loads[1].wait()
+        loads[2].wait()
+        blocks(block_states)
+        fill(f_sb, kv)
+
+    def do_scores():
+        loads[3].wait()
+        blocks(scores)
+
+    def do_own():
+        for b in range(BLOCKS):
+            own[rows(b), :] = dot(normed[rows(b), :], w[:, columns(y)])
+
+    def do_back_mix():
+        blocks(back_mix)
+        fill(b_sb, gkv)
+
+    def do_back_local():
+        blocks(back_local)
+
+    def do_back_end():
+        blocks(back_end)
+
+    steps = {
+        "go": loads[0].wait,
+        "weight": loads[4].wait,
+        "meet": lambda: pl.semaphore_wait(barrier, 2 + N_ROW - 1 + N_Z - 1),
+        "states": do_states,
+        "scores": do_scores,
+        "mix": lambda: blocks(mix),
+        "rest": do_rest,
+        "near": do_near,
+        "far": do_far,
+        "back_mix": do_back_mix,
+        "back_local": do_back_local,
+        "back_end": do_back_end,
+        "own": do_own,
+        "part_far": lambda: partial(2, y_far),
+        "part_next": lambda: partial(0, y_next),
+        "part_prev": lambda: partial(1, y_prev),
+        "f1": lambda: scan_start(0, f_sb, f_rb),
+        "f2": lambda: scan_middle(0, f_rb, f_zs, f_zb),
+        "f3": lambda: scan_late(0, f_rb, f_zb, f_pb, f_fb, False),
+        "f4": lambda: scan_end(0, f_fb),
+        "b1": lambda: scan_start(1, b_sb, b_rb),
+        "b2": lambda: scan_middle(1, b_rb, b_zs, b_zb),
+        "b3": lambda: scan_late(1, b_rb, b_zb, b_pb, b_fb, True),
+        "b4": lambda: scan_end(1, b_fb),
+    }
     for b in range(BLOCKS):
-        for way in range(2):
-            ag_own(b, way).wait_send()
-            ag_relay(b, way).wait_send()
-            rs_first(b, way).wait_send()
-            rs_plain(b, way).wait_send()
-            rs_added(b, way).wait_send()
-    scan_sent(0, f_sb, f_rb, f_zs, f_zb, f_pb, f_fb)
-    scan_sent(1, b_sb, b_rb, b_zs, b_zb, b_pb, b_fb)
+        steps[f"mask{b}"] = functools.partial(mask, b)
+        steps[f"send{b}"] = functools.partial(do_send, b)
+        steps[f"relay{b}"] = functools.partial(do_relay, b)
+        steps[f"add{b}"] = functools.partial(add_relayed, b)
+        steps[f"fin{b}"] = functools.partial(finish, b)
     for j in range(4):
-        w_sent(j)
-        w_store(j, True).wait()
-        w_store(j, False).wait()
-    for store in stores:
-        store.wait()
+        steps[f"gn{j}"] = functools.partial(grad_normed, j)
+        for n, act in enumerate((w_start, w_x, w_z, w_turn, w_x_back, w_core_back, w_end)):
+            steps[f"w{n}_{j}"] = functools.partial(act, j)
+    for name in ORDER:
+        steps[name]()
+
+    for wait in sent:
+        wait()
+
+
+def write_out(*refs):
+    sources, targets, done = refs[:5], refs[5:10], refs[10]
+    copies = [
+        pltpu.make_async_copy(a, b, done.at[i]) for i, (a, b) in enumerate(zip(sources, targets))
+    ]
+    for copy in copies:
+        copy.start()
+    for copy in copies:
+        copy.wait()
 
 
 def local(queries, attn_keys, attn_values, out_weight, grad_out, drop_seed):
@@ -662,7 +640,6 @@
         vmem(square, BF16),
         vmem((BLOCKS, HEADS, HD, HD), F32),
         vmem(square, F32), vmem(square, F32),
-        vmem(square, BF16), vmem(square, BF16), vmem(square, BF16), vmem(square, BF16),
         *scan_buffers, *scan_buffers,
         vmem((4, 256, 512), BF16),
         vmem((4, 256, 512), F32),
@@ -675,8 +652,8 @@
         vmem((4, 8, 16, 256), BF16),
         vmem((4, 4, 64, 512), BF16),
         vmem((4, 4, 64, 512), BF16),
-        dma((5,)), dma((12,)),
-        dma((2, 3)), dma((2, 3)), dma((2, 3)), dma((2, 3)),
+        dma((5,)),
+        dma((2, 2, 3)), dma((2, 2, 3)), dma((2, 3)), dma((2, 3)),
         dma((2, 3, 3)), dma((2, 3, 3)),
         dma((2, 3, 8)), dma((2, 3, 8)),
         dma((2, 4)), dma((2, 4)),
@@ -686,20 +663,27 @@
     hbm = pl.BlockSpec(memory_space=pl.ANY)
     outs = pl.pallas_call(
         kernel,
-        out_shape=[jax.ShapeDtypeStruct(square, BF16)] * 4
-        + [jax.ShapeDtypeStruct((8, 64, MODEL), BF16)],
+        out_shape=[vmem(square, BF16)] * 4 + [vmem((8, 64, MODEL), BF16)],
         in_specs=[pl.BlockSpec(memory_space=pltpu.SMEM)] + [hbm] * 5,
-        out_specs=[hbm] * 5,
+        out_specs=[pl.BlockSpec(memory_space=vmem)] * 5,
         scratch_shapes=scratch,
         compiler_params=pltpu.CompilerParams(
-            collective_id=0, has_side_effects=True, vmem_limit_bytes=60 * 1024 * 1024
+            collective_id=0, has_side_effects=True, vmem_limit_bytes=56 * 1024 * 1024
         ),
         cost_estimate=pl.CostEstimate(
             flops=7_000_000_000, bytes_accessed=11_000_000, transcendentals=3072
         ),
         name="layer",
     )(drop_seed, queries, attn_keys, attn_values, out_weight, grad_out)
-    output, grad_q, grad_k, grad_v, grad_w = outs
+    output, grad_q, grad_k, grad_v, grad_w = pl.pallas_call(
+        write_out,
+        out_shape=[jax.ShapeDtypeStruct(square, BF16)] * 4
+        + [jax.ShapeDtypeStruct((8, 64, MODEL), BF16)],
+        in_specs=[pl.BlockSpec(memory_space=vmem)] * 5,
+        out_specs=[hbm] * 5,
+        scratch_shapes=[dma((5,))],
+        name="write_out",
+    )(*outs)
     return output, grad_q, grad_k, grad_v, grad_w.reshape(WIDTH, MODEL)
 
 

time: 95 us -> 85.5 us (0.900)
  Pallas kernels: 87.4 us -> 79.2 us
  local copies, waits for them, and re-layouts: 6.19 us -> 4.89 us
    pallas_call x1 -> x2, Pallas kernels: 87.4 us -> 79.2 us  [the longest x1 74.2 us: local(): pl.pallas_call(kernel, out_shape=[vmem(square, BF16)] * 4 + [vmem((8, 64,...]
    unnamed x13 -> x10, local copies, waits for them, and re-layouts: 6.19 us -> 4.89 us
where the time goes in v2:
time: 85.5 us; the launch traced here: 85.4 us
  Pallas kernels  79.2 us (93%)
  local copies, waits for them, and re-layouts  4.89 us (6%)
  between operations  1.3 us (2%)
    pallas_call x1, Pallas kernels, local(): pl.pallas_call(kernel, out_shape=[vmem(square, BF16)] * 4 + [vmem((8, 64,...  74.2 us
    pallas_call x1, Pallas kernels, local(): pl.pallas_call(write_out, out_shape=[jax.ShapeDtypeStruct(square, BF16)]...  4.95 us
    unnamed x10, local copies, waits for them, and re-layouts  4.89 us

profile of v2, /device:TPU:1, one launch (start us, length us, event | category | flops | bytes accessed | tf_op | source)
XLA Modules:
  0.0 85.4 jit_solution(6079460736917042897)
XLA Ops:
  1.3 74.2 %layer.1 = (bf16[768,512]{1,0:T(8,128)(2,1)S(1)}, bf16[768,512]{1,0:T(8,128)(2,1)S(1)}, bf16[768,512]{1,0:T(8,128)(2,1)S(1)}, bf16[768,512]{1,0:T(8,128)(2,1)S(1)}, bf16[8,64,2048]{2,1,0:T(8,128)(2,1)S(1)}) custom-call(s32[1]{0:T(128)S(6)} %copy.11.seed_ref, bf16[768,512]{1,0:T(8,128)(2,1)} %q_hbm.1, bf16[768,512]{1,0:T(8,128)(2,1)} %k_hbm.1, ...), custom_call_target="tpu_custom_call" | custom-call | flops 7000000000 | bytes 11000000 | tf_op jit(solution)/shard_map/layer/pallas_call | solution.py:664
  75.5 0.0 copy-start
  75.5 1.3 %copy-done = bf16[8,64,2048]{2,1,0:T(8,128)(2,1)} copy-done((bf16[8,64,2048]{2,1,0:T(8,128)(2,1)}, bf16[8,64,2048]{2,1,0:T(8,128)(2,1)S(1)}, u32[]{:S(2)}) %copy-start) | copy-done | bytes 2097176
  76.9 0.0 copy-start.1
  76.9 0.9 %copy-done.1 = bf16[768,512]{1,0:T(8,128)(2,1)} copy-done((bf16[768,512]{1,0:T(8,128)(2,1)}, bf16[768,512]{1,0:T(8,128)(2,1)S(1)}, u32[]{:S(2)}) %copy-start.1) | copy-done | bytes 786456
  77.7 0.0 copy-start.2
  77.7 0.9 %copy-done.2 = bf16[768,512]{1,0:T(8,128)(2,1)} copy-done((bf16[768,512]{1,0:T(8,128)(2,1)}, bf16[768,512]{1,0:T(8,128)(2,1)S(1)}, u32[]{:S(2)}) %copy-start.2) | copy-done | bytes 786456
  78.6 0.0 copy-start.3
  78.6 0.9 %copy-done.3 = bf16[768,512]{1,0:T(8,128)(2,1)} copy-done((bf16[768,512]{1,0:T(8,128)(2,1)}, bf16[768,512]{1,0:T(8,128)(2,1)S(1)}, u32[]{:S(2)}) %copy-start.3) | copy-done | bytes 786456
  79.5 0.0 copy-start.4
  79.5 0.9 %copy-done.4 = bf16[768,512]{1,0:T(8,128)(2,1)} copy-done((bf16[768,512]{1,0:T(8,128)(2,1)}, bf16[768,512]{1,0:T(8,128)(2,1)S(1)}, u32[]{:S(2)}) %copy-start.4) | copy-done | bytes 786456
  80.4 5.0 %write_out.1 = (bf16[768,512]{1,0:T(8,128)(2,1)}, bf16[768,512]{1,0:T(8,128)(2,1)}, bf16[768,512]{1,0:T(8,128)(2,1)}, bf16[768,512]{1,0:T(8,128)(2,1)}, bf16[8,64,2048]{2,1,0:T(8,128)(2,1)}) custom-call(bf16[768,512]{1,0:T(8,128)(2,1)} %copy-done.1, bf16[768,512]{1,0:T(8,128)(2,1)} %copy-done.2, bf16[768,512]{1,0:T(8,128)(2,1)} %copy-done.3, ...), custom_call_target="tpu_custom_call" | custom-call | tf_op jit(solution)/shard_map/write_out/pallas_call | solution.py:678
Async XLA Ops:
  75.5 1.4 %copy-start = (bf16[8,64,2048]{2,1,0:T(8,128)(2,1)}, bf16[8,64,2048]{2,1,0:T(8,128)(2,1)S(1)}, u32[]{:S(2)}) copy-start(bf16[8,64,2048]{2,1,0:T(8,128)(2,1)S(1)} %get-tuple-element.19.refs_4_) | copy-start | bytes 6291460
  76.9 0.9 %copy-start.1 = (bf16[768,512]{1,0:T(8,128)(2,1)}, bf16[768,512]{1,0:T(8,128)(2,1)S(1)}, u32[]{:S(2)}) copy-start(bf16[768,512]{1,0:T(8,128)(2,1)S(1)} %get-tuple-element.15.refs_0_) | copy-start | bytes 2359300
  77.7 0.9 %copy-start.2 = (bf16[768,512]{1,0:T(8,128)(2,1)}, bf16[768,512]{1,0:T(8,128)(2,1)S(1)}, u32[]{:S(2)}) copy-start(bf16[768,512]{1,0:T(8,128)(2,1)S(1)} %get-tuple-element.16.refs_1_) | copy-start | bytes 2359300
  78.6 0.9 %copy-start.3 = (bf16[768,512]{1,0:T(8,128)(2,1)}, bf16[768,512]{1,0:T(8,128)(2,1)S(1)}, u32[]{:S(2)}) copy-start(bf16[768,512]{1,0:T(8,128)(2,1)S(1)} %get-tuple-element.17.refs_2_) | copy-start | bytes 2359300
  79.5 0.9 %copy-start.4 = (bf16[768,512]{1,0:T(8,128)(2,1)}, bf16[768,512]{1,0:T(8,128)(2,1)S(1)}, u32[]{:S(2)}) copy-start(bf16[768,512]{1,0:T(8,128)(2,1)S(1)} %get-tuple-element.18.refs_3_) | copy-start | bytes 2359300

commit v3 on v2

--- a/solution.py
+++ b/solution.py
@@ -36,12 +36,10 @@
 
 ORDER = (
     "go", "mask0", "states", "meet", "f1", "send0", "mask1", "send1", "mask2", "send2", "rest",
-    "f2", "scores", "f3", "weight", "gn0", "relay0", "relay1", "relay2", "f4", "mix",
-    "part_far", "w0_0", "part_next", "part_prev", "w1_0",
-    "own", "w2_0", "near", "w0_1", "w0_2", "gn1", "gn2", "w1_1", "w1_2",
-    "far", "gn3", "back_mix", "b1", "w0_3", "w3_0", "w1_3", "w2_1", "w2_2", "b2", "add0", "add1", "add2", "w2_3", "w4_0", "back_local",
-    "w3_1", "w3_2", "b3", "w3_3", "w5_0", "w4_1", "w4_2", "b4", "back_end", "w4_3", "w6_0", "w5_1", "w5_2",
-    "w5_3", "w6_1", "w6_2", "fin0", "fin1", "fin2", "w6_3",
+    "f2", "scores", "f3", "weight", "gn0", "f4", "relay0", "relay1", "relay2", "mix",
+    "w0_0", "part_far", "part_next", "part_prev", "w1_0", "near", "w0_1", "w0_2", "gn1", "gn2", "own", "w1_1", "w1_2", "w2_0",
+    "far0", "far1", "far2", "w0_3", "fill", "b1", "w1_3", "w2_1", "w2_2", "w3_0", "add0", "add1", "add2", "b2", "local0", "w2_3", "w4_0", "w3_1", "w3_2",
+    "local1", "b3", "local2", "w3_3", "w4_1", "w4_2", "w5_0", "b4", "back_end", "w4_3", "w5_1", "w5_2", "w6_0", "w6_1", "w6_2", "fin0", "w5_3", "fin1", "fin2", "w6_3",
 )
 
 
@@ -81,14 +79,13 @@
 
 
 def kernel(
-    seed_ref, q_hbm, k_hbm, v_hbm, w_hbm, go_hbm,
+    seed_hbm, q_hbm, k_hbm, v_hbm, w_hbm, go_hbm,
     out_b, gq_b, gk_b, gv_b, gw_out,
     q, k, v, go, w, scale, gp, kv, cs, state, mixed, inv, normed, turned,
     ps, own, relay_in, rin, gn, gm, gkv, gk_acc, gv_acc,
     f_sb, f_rb, f_zs, f_zb, f_pb, f_fb, b_sb, b_rb, b_zs, b_zb, b_pb, b_fb,
-    wsend, wown, wrecv, xs, xb, zsw, zbw, zone, zg, xg, pg,
-    load_sem, ag_s, ag_r, agr_s, agr_r, rs_s, rs_r,
-    scan_s, scan_r, core_s, core_r, wx_s, wx_r, wz_s, wz_r,
+    seed_ref, wsend, wown, wrecv, xs, xb, zsw, zbw, zone, zg, xg, pg,
+    load_sem, ag_s, ag_r, rs_s, rs_r, scan_s, scan_r, w_s, w_r,
 ):
     seq = lax.axis_index("seq")
     y = lax.axis_index("head")
@@ -120,8 +117,6 @@
             device_id=device, device_id_type=MESH,
         )
 
-    sent = []
-
     def loop(count, act):
         def step(i, _):
             act(i)
@@ -131,67 +126,66 @@
 
     def start(copy):
         copy.start()
-        sent.append(copy.wait_send)
 
     def start_all(count, make):
         loop(count, lambda i: make(i).start())
-        sent.append(lambda: loop(count, lambda i: make(i).wait_send()))
-
-    def put(copy):
-        copy.start()
-        sent.append(copy.wait)
-
-    def arrive(copy):
-        copy.wait_recv()
-
-    def arrive_all(count, make):
-        loop(count, lambda i: make(i).wait_recv())
+
+    def arrive(ref, sem):
+        remote(ref, ref, sem, sem, partner).wait_recv()
+
+    def left(ref, sem):
+        remote(ref, ref, sem, sem, partner).wait_send()
+
+    barrier = pltpu.get_barrier_semaphore()
+    for device in beside:
+        pl.semaphore_signal(barrier, inc=1, device_id=device, device_id_type=MESH)
+
+    def greet(i, _):
+        pl.semaphore_signal(
+            barrier, inc=1, device_id=at(z, row_peer(i), y), device_id_type=MESH
+        )
+        pl.semaphore_signal(
+            barrier, inc=1, device_id=at(z_peer(i), r, y), device_id_type=MESH
+        )
+        return 0
+
+    lax.fori_loop(1, N_ROW, greet, 0)
 
     loads = [
         pltpu.make_async_copy(a, b, load_sem.at[i])
         for i, (a, b) in enumerate(
-            ((go_hbm, go), (k_hbm, k), (v_hbm, v), (q_hbm, q), (w_hbm, w))
+            (
+                (go_hbm, go), (k_hbm, k), (v_hbm, v), (q_hbm, q), (w_hbm, w),
+                (seed_hbm, seed_ref),
+            )
         )
     ]
-    for load in loads:
+    loads[5].start()
+    for load in loads[:5]:
         load.start()
-
-    barrier = pltpu.get_barrier_semaphore()
-    for device in beside:
-        pl.semaphore_signal(barrier, inc=1, device_id=device, device_id_type=MESH)
-
-    def greet(i, _):
-        pl.semaphore_signal(
-            barrier, inc=1, device_id=at(z, row_peer(i), y), device_id_type=MESH
-        )
-        pl.semaphore_signal(
-            barrier, inc=1, device_id=at(z_peer(i), r, y), device_id_type=MESH
-        )
-        return 0
-
-    lax.fori_loop(1, N_ROW, greet, 0)
 
     def ag_own(b, way, late):
         part = half_rows(b, 1 - way if late else way)
         return remote(
-            gp.at[0, part], gp.at[1 + way, part], ag_s.at[way, late, b], ag_r.at[way, late, b],
+            gp.at[0, part], gp.at[1 + way, part], ag_s.at[0], ag_r.at[3 if late else b],
             beside[way],
         )
 
     def ag_relay(b, way):
         part = half_rows(b, way)
         return remote(
-            gp.at[1 + way, part], gp.at[3, part], agr_s.at[way, b], agr_r.at[way, b],
+            gp.at[1 + way, part], gp.at[3, part], ag_s.at[1], ag_r.at[4 + b],
             beside[way],
         )
 
-    seed = seed_ref[0]
     first_row = seq * ROWS
     first_column = y * WIDTH
     features = first_column + lax.broadcasted_iota(jnp.int32, (1, WIDTH), 1)
     TILE = 16
 
     def mask(b):
+        seed = seed_ref[0]
+
         def step(i, _):
             start = pl.multiple_of(b * SPAN + i * TILE, TILE)
             positions = first_row + start + lax.broadcasted_iota(jnp.int32, (TILE, 1), 0)
@@ -217,33 +211,22 @@
 
     def scan_one(n, i, sb, rb):
         t = row_peer(i)
-        return remote(sb.at[t], rb.at[r], scan_s.at[n, 0, i], scan_r.at[n, 0, i], at(z, t, y))
+        return remote(sb.at[t], rb.at[r], scan_s.at[n, 0], scan_r.at[n, 0], at(z, t, y))
 
     def scan_two(n, i, zs, zb):
         t = z_peer(i)
-        return remote(zs, zb.at[z], scan_s.at[n, 1, i], scan_r.at[n, 1, i], at(t, r, y))
+        return remote(zs, zb.at[z], scan_s.at[n, 1], scan_r.at[n, 1], at(t, r, y))
 
     def scan_three(n, i, pb, fb):
         t = row_peer(i)
-        return remote(pb.at[t], fb.at[r], scan_s.at[n, 2, i], scan_r.at[n, 2, i], at(z, t, y))
-
-    def row_from(i):
-        return (r + N_ROW - i) % N_ROW
-
-    def z_from(i):
-        return (z + N_Z - i) % N_Z
-
-    def x_from(i):
-        return (x + N_X - i) % N_X
+        return remote(pb.at[t], fb.at[r], scan_s.at[n, 2], scan_r.at[n, 2], at(z, t, y))
 
     def scan_start(n, sb, rb):
         rb[r] = sb[r]
         start_all(N_ROW, lambda i: scan_one(n, i, sb, rb))
 
     def scan_middle(n, rb, zs, zb):
-        arrive_all(N_ROW, lambda i: remote(
-                rb.at[0], rb.at[row_from(i)], scan_s.at[n, 0, i], scan_r.at[n, 0, i], partner
-            ))
+        arrive(rb.at[pl.ds(0, N_ROW - 1)], scan_r.at[n, 0])
         total = rb[0].astype(F32)
         for j in range(1, N_ROW):
             total = total + rb[j].astype(F32)
@@ -253,9 +236,7 @@
         start_all(N_Z, lambda i: scan_two(n, i, zs, zb))
 
     def scan_late(n, rb, zb, pb, fb, reverse):
-        arrive_all(N_Z, lambda i: remote(
-                zb.at[0], zb.at[z_from(i)], scan_s.at[n, 1, i], scan_r.at[n, 1, i], partner
-            ))
+        arrive(zb.at[pl.ds(0, N_Z - 1)], scan_r.at[n, 1])
         run = jnp.zeros((HD // 2, HD), F32)
         for j in range(N_Z):
             wanted = (j > z) if reverse else (j < z)
@@ -268,9 +249,7 @@
         start_all(N_ROW, lambda i: scan_three(n, i, pb, fb))
 
     def scan_end(n, fb):
-        arrive_all(N_ROW, lambda i: remote(
-                fb.at[0], fb.at[row_from(i)], scan_s.at[n, 2, i], scan_r.at[n, 2, i], partner
-            ))
+        arrive(fb.at[pl.ds(0, N_ROW - 1)], scan_r.at[n, 2])
 
     causal = lax.broadcasted_iota(jnp.int32, (SPAN, SPAN), 0) >= lax.broadcasted_iota(
         jnp.int32, (SPAN, SPAN), 1
@@ -290,11 +269,14 @@
 
     model_block = (y, y_prev, y_next, y_far)
 
+    def add_grad_normed(slot, b):
+        at_rows = pl.ds(pl.multiple_of(b * SPAN, SPAN), SPAN)
+        term = dot(gp[slot, at_rows, :], w[:, columns(model_block[slot])], NT)
+        gn[at_rows, :] = term if slot == 0 else gn[at_rows, :] + term
+
     def grad_normed(slot):
         def go_on(b, _):
-            at_rows = pl.ds(pl.multiple_of(b * SPAN, SPAN), SPAN)
-            term = dot(gp[slot, at_rows, :], w[:, columns(model_block[slot])], NT)
-            gn[at_rows, :] = term if slot == 0 else gn[at_rows, :] + term
+            add_grad_normed(slot, b)
             return 0
 
         lax.fori_loop(0, BLOCKS, go_on, 0)
@@ -319,20 +301,20 @@
     def rs_first(b, way):
         return remote(
             ps.at[2, half_rows(b, way)], relay_in.at[way, b],
-            rs_s.at[way, 0, b], rs_r.at[way, 0, b], beside[way],
+            rs_s.at[0], rs_r.at[b], beside[way],
         )
 
     def rs_plain(b, way):
         part = half_rows(b, 1 - way)
         return remote(
-            ps.at[way, part], rin.at[way, part], rs_s.at[way, 1, b], rs_r.at[way, 1, b],
+            ps.at[way, part], rin.at[way, part], rs_s.at[1], rs_r.at[3 + b],
             beside[way],
         )
 
     def rs_added(b, way):
         part = half_rows(b, way)
         return remote(
-            ps.at[way, part], rin.at[way, part], rs_s.at[way, 2, b], rs_r.at[way, 2, b],
+            ps.at[way, part], rin.at[way, part], rs_s.at[1], rs_r.at[3 + b],
             beside[way],
         )
 
@@ -348,32 +330,32 @@
     half = WIDTH // 2
 
     def core_out(j):
-        return remote(wsend.at[j], wrecv.at[j], core_s.at[0, j], core_r.at[0, j], partner)
+        return remote(wsend.at[j], wrecv.at[j], w_s.at[0], w_r.at[0, j], partner)
 
     def core_back(j):
-        return remote(xg.at[j], pg.at[j], core_s.at[1, j], core_r.at[1, j], partner)
+        return remote(xg.at[j], pg.at[j], w_s.at[1], w_r.at[1, j], partner)
 
     def x_out(j, i):
         t = x_peer(i)
         return remote(
-            xs.at[j, t], xb.at[j, x], wx_s.at[0, j, i], wx_r.at[0, j, i], at(z, t * 2 + c, y)
+            xs.at[j, t], xb.at[j, x], w_s.at[2], w_r.at[2, j], at(z, t * 2 + c, y)
         )
 
     def x_back(j, i):
         t = x_peer(i)
         return remote(
-            xg.at[j, x], xg.at[j, x], wx_s.at[1, j, i], wx_r.at[1, j, i], at(z, t * 2 + c, y)
+            xg.at[j, x], xg.at[j, x], w_s.at[3], w_r.at[3, j], at(z, t * 2 + c, y)
         )
 
     def z_out(j, i):
         t = z_peer(i)
         return remote(
-            zsw.at[j, t], zbw.at[j, z], wz_s.at[0, j, i], wz_r.at[0, j, i], at(t, r, y)
+            zsw.at[j, t], zbw.at[j, z], w_s.at[4], w_r.at[4, j], at(t, r, y)
         )
 
     def z_back(j, i):
         t = z_peer(i)
-        return remote(zone.at[j], zg.at[j, z], wz_s.at[1, j, i], wz_r.at[1, j, i], at(t, r, y))
+        return remote(zone.at[j], zg.at[j, z], w_s.at[5], w_r.at[5, j], at(t, r, y))
 
     def w_start(j):
         theirs = pl.ds(pl.multiple_of(other * half, half), half)
@@ -383,7 +365,7 @@
         wown[j] = dot(turned[mine, :], gp[j])
 
     def w_x(j):
-        arrive(core_out(j))
+        arrive(wrecv.at[j], w_r.at[0, j])
         for t in range(N_X):
             part = pl.ds(t * 64, 64)
             xs[j, t] = (wown[j, part, :] + wrecv[j, part, :].astype(F32)).astype(BF16)
@@ -391,9 +373,7 @@
         start_all(N_X, lambda i: x_out(j, i))
 
     def w_z(j):
-        arrive_all(N_X, lambda i: remote(
-                xs.at[j, 0], xb.at[j, x_from(i)], wx_s.at[0, j, i], wx_r.at[0, j, i], partner
-            ))
+        arrive(xb.at[j, pl.ds(0, N_X - 1)], w_r.at[2, j])
         total = xb[j, 0].astype(F32)
         for t in range(1, N_X):
             total = total + xb[j, t].astype(F32)
@@ -404,9 +384,7 @@
         start_all(N_Z, lambda i: z_out(j, i))
 
     def w_turn(j):
-        arrive_all(N_Z, lambda i: remote(
-                zsw.at[j, 0], zbw.at[j, z_from(i)], wz_s.at[0, j, i], wz_r.at[0, j, i], partner
-            ))
+        arrive(zbw.at[j, pl.ds(0, N_Z - 1)], w_r.at[4, j])
         total = zbw[j, 0].astype(F32)
         for t in range(1, N_Z):
             total = total + zbw[j, t].astype(F32)
@@ -416,9 +394,7 @@
         start_all(N_Z, lambda i: z_back(j, i))
 
     def w_x_back(j):
-        arrive_all(N_Z, lambda i: remote(
-                zone.at[j], zg.at[j, z_from(i)], wz_s.at[1, j, i], wz_r.at[1, j, i], partner
-            ))
+        arrive(zg.at[j, pl.ds(0, N_Z - 1)], w_r.at[5, j])
         pieces = [
             jnp.concatenate([zg[j, 2 * t], zg[j, 2 * t + 1]], axis=1) for t in range(N_Z // 2)
         ]
@@ -432,14 +408,12 @@
             gw_out[first + t, :, columns(model_block[j])] = source[j, t]
 
     def w_core_back(j):
-        arrive_all(N_X, lambda i: remote(
-                xg.at[j, 0], xg.at[j, x_from(i)], wx_s.at[1, j, i], wx_r.at[1, j, i], partner
-            ))
+        arrive(xg.at[j, pl.ds(0, N_X - 1)], w_r.at[3, j])
         start(core_back(j))
         w_store(j, True)
 
     def w_end(j):
-        arrive(core_back(j))
+        arrive(pg.at[j], w_r.at[1, j])
         w_store(j, False)
 
     def back_mix(b, _):
@@ -455,8 +429,8 @@
         return 0
 
     def add_relayed(b):
+        arrive(relay_in.at[:, b], rs_r.at[b])
         for way in range(2):
-            arrive(rs_first(b, way))
             part = half_rows(b, way)
             both = ps[way, part, :].astype(F32) + relay_in[way, b].astype(F32)
             ps[way, part, :] = both.astype(BF16)
@@ -491,9 +465,7 @@
         return 0
 
     def finish(b):
-        for way in range(2):
-            arrive(rs_plain(b, way))
-            arrive(rs_added(b, way))
+        arrive(rin.at[:, rows(b)], rs_r.at[3 + b])
 
         def step(i, _):
             at_rows = pl.ds(pl.multiple_of(b * SPAN + i * 32, 32), 32)
@@ -516,19 +488,15 @@
                 start(ag_own(b, way, 1))
 
     def do_relay(b):
+        arrive(gp.at[1, rows(b)], ag_r.at[b])
         for way in range(2):
-            arrive(ag_own(b, way, 0))
             start(ag_relay(b, way))
 
     def do_near():
-        for b in range(BLOCKS):
-            for way in range(2):
-                arrive(ag_own(b, way, 1))
-
-    def do_far():
-        for b in range(BLOCKS):
-            for way in range(2):
-                arrive(ag_relay(b, way))
+        arrive(gp.at[1], ag_r.at[3])
+
+    def do_far(b):
+        arrive(gp.at[3, rows(b)], ag_r.at[4 + b])
 
     def do_states():
         loads[1].wait()
@@ -544,18 +512,16 @@
         for b in range(BLOCKS):
             own[rows(b), :] = dot(normed[rows(b), :], w[:, columns(y)])
 
-    def do_back_mix():
-        blocks(back_mix)
-        fill(b_sb, gkv)
-
-    def do_back_local():
-        blocks(back_local)
+    def do_far_mix(b):
+        do_far(b)
+        add_grad_normed(3, b)
+        back_mix(b, 0)
 
     def do_back_end():
         blocks(back_end)
 
     steps = {
-        "go": loads[0].wait,
+        "go": lambda: (loads[5].wait(), loads[0].wait()),
         "weight": loads[4].wait,
         "meet": lambda: pl.semaphore_wait(barrier, 2 + N_ROW - 1 + N_Z - 1),
         "states": do_states,
@@ -563,9 +529,7 @@
         "mix": lambda: blocks(mix),
         "rest": do_rest,
         "near": do_near,
-        "far": do_far,
-        "back_mix": do_back_mix,
-        "back_local": do_back_local,
+        "fill": lambda: fill(b_sb, gkv),
         "back_end": do_back_end,
         "own": do_own,
         "part_far": lambda: partial(2, y_far),
@@ -585,7 +549,9 @@
         steps[f"send{b}"] = functools.partial(do_send, b)
         steps[f"relay{b}"] = functools.partial(do_relay, b)
         steps[f"add{b}"] = functools.partial(add_relayed, b)
+        steps[f"local{b}"] = functools.partial(back_local, b, 0)
         steps[f"fin{b}"] = functools.partial(finish, b)
+        steps[f"far{b}"] = functools.partial(do_far_mix, b)
     for j in range(4):
         steps[f"gn{j}"] = functools.partial(grad_normed, j)
         for n, act in enumerate((w_start, w_x, w_z, w_turn, w_x_back, w_core_back, w_end)):
@@ -593,8 +559,20 @@
     for name in ORDER:
         steps[name]()
 
-    for wait in sent:
-        wait()
+    left(gp.at[pl.ds(0, 2)], ag_s.at[0])
+    left(gp.at[3], ag_s.at[1])
+    left(ps.at[2], rs_s.at[0])
+    left(ps.at[pl.ds(0, 2)], rs_s.at[1])
+    for n, (eight, zs) in enumerate(((f_rb, f_zb), (b_rb, b_zb))):
+        left(eight.at[pl.ds(0, N_ROW - 1)], scan_s.at[n, 0])
+        left(zs.at[pl.ds(0, N_Z - 1)], scan_s.at[n, 1])
+        left(eight.at[pl.ds(0, N_ROW - 1)], scan_s.at[n, 2])
+    left(wsend, w_s.at[0])
+    left(xg, w_s.at[1])
+    left(xs.at[:, pl.ds(0, N_X - 1)], w_s.at[2])
+    left(xg.at[:, pl.ds(0, N_X - 1)], w_s.at[3])
+    left(zsw.at[:, pl.ds(0, N_Z - 1)], w_s.at[4])
+    left(zg.at[:, pl.ds(0, N_Z - 1)], w_s.at[5])
 
 
 def write_out(*refs):
@@ -641,6 +619,7 @@
         vmem((BLOCKS, HEADS, HD, HD), F32),
         vmem(square, F32), vmem(square, F32),
         *scan_buffers, *scan_buffers,
+        pltpu.SMEM((1,), jnp.int32),
         vmem((4, 256, 512), BF16),
         vmem((4, 256, 512), F32),
         vmem((4, 256, 512), BF16),
@@ -652,19 +631,17 @@
         vmem((4, 8, 16, 256), BF16),
         vmem((4, 4, 64, 512), BF16),
         vmem((4, 4, 64, 512), BF16),
-        dma((5,)),
-        dma((2, 2, 3)), dma((2, 2, 3)), dma((2, 3)), dma((2, 3)),
-        dma((2, 3, 3)), dma((2, 3, 3)),
-        dma((2, 3, 8)), dma((2, 3, 8)),
-        dma((2, 4)), dma((2, 4)),
-        dma((2, 4, 4)), dma((2, 4, 4)),
-        dma((2, 4, 8)), dma((2, 4, 8)),
+        dma((6,)),
+        dma((2,)), dma((7,)),
+        dma((2,)), dma((6,)),
+        dma((2, 3)), dma((2, 3)),
+        dma((6,)), dma((6, 4)),
     ]
     hbm = pl.BlockSpec(memory_space=pl.ANY)
     outs = pl.pallas_call(
         kernel,
         out_shape=[vmem(square, BF16)] * 4 + [vmem((8, 64, MODEL), BF16)],
-        in_specs=[pl.BlockSpec(memory_space=pltpu.SMEM)] + [hbm] * 5,
+        in_specs=[hbm] * 6,
         out_specs=[pl.BlockSpec(memory_space=vmem)] * 5,
         scratch_shapes=scratch,
         compiler_params=pltpu.CompilerParams(
@@ -682,6 +659,7 @@
         in_specs=[pl.BlockSpec(memory_space=vmem)] * 5,
         out_specs=[hbm] * 5,
         scratch_shapes=[dma((5,))],
+        compiler_params=pltpu.CompilerParams(vmem_limit_bytes=1024 * 1024),
         name="write_out",
     )(*outs)
     return output, grad_q, grad_k, grad_v, grad_w.reshape(WIDTH, MODEL)

time: 85.5 us -> 72.3 us (0.85)
  Pallas kernels: 79.2 us -> 70.9 us
  local copies, waits for them, and re-layouts: 4.89 us -> 0 us
    pallas_call x1, Pallas kernels: 74.2 us -> 68.5 us  [local(): pl.pallas_call(kernel, out_shape=[vmem(square, BF16)] * 4 + [vmem((8, 64,...]
    unnamed x10 -> x0, local copies, waits for them, and re-layouts: 4.89 us -> none
    pallas_call x1, Pallas kernels: 4.95 us -> 2.4 us  [local(): pl.pallas_call(write_out, out_shape=[jax.ShapeDtypeStruct(square, BF16)]...]
where the time goes in v3:
time: 72.3 us; the launch traced here: 72.2 us
  Pallas kernels  70.9 us (98%)
  between operations  1.29 us (2%)
    pallas_call x1, Pallas kernels, local(): pl.pallas_call(kernel, out_shape=[vmem(square, BF16)] * 4 + [vmem((8, 64,...  68.5 us
    pallas_call x1, Pallas kernels, local(): pl.pallas_call(write_out, out_shape=[jax.ShapeDtypeStruct(square, BF16)]...  2.4 us

profile of v3, /device:TPU:1, one launch (start us, length us, event | category | flops | bytes accessed | tf_op | source)
XLA Modules:
  0.0 72.2 jit_solution(2295892978851287775)
XLA Ops:
  1.3 68.5 %layer.1 = (bf16[768,512]{1,0:T(8,128)(2,1)S(1)}, bf16[768,512]{1,0:T(8,128)(2,1)S(1)}, bf16[768,512]{1,0:T(8,128)(2,1)S(1)}, bf16[768,512]{1,0:T(8,128)(2,1)S(1)}, bf16[8,64,2048]{2,1,0:T(8,128)(2,1)S(1)}) custom-call(s32[1]{0:T(128)S(6)} %copy.11.seed_hbm, bf16[768,512]{1,0:T(8,128)(2,1)} %q_hbm.1, bf16[768,512]{1,0:T(8,128)(2,1)} %k_hbm.1, ...), custom_call_target="tpu_custom_call" | custom-call | flops 7000000000 | bytes 11000000 | tf_op jit(solution)/shard_map/layer/pallas_call | solution.py:641
  69.8 2.4 %write_out.1 = (bf16[768,512]{1,0:T(8,128)(2,1)}, bf16[768,512]{1,0:T(8,128)(2,1)}, bf16[768,512]{1,0:T(8,128)(2,1)}, bf16[768,512]{1,0:T(8,128)(2,1)}, bf16[8,64,2048]{2,1,0:T(8,128)(2,1)}) custom-call(bf16[768,512]{1,0:T(8,128)(2,1)S(1)} %get-tuple-element.15.refs_0_, bf16[768,512]{1,0:T(8,128)(2,1)S(1)} %get-tuple-element.16.refs_1_, ...), custom_call_target="tpu_custom_call" | custom-call | tf_op jit(solution)/shard_map/write_out/pallas_call | solution.py:655

commit v4 on v3

--- a/solution.py
+++ b/solution.py
@@ -35,11 +35,10 @@
 
 
 ORDER = (
-    "go", "mask0", "states", "meet", "f1", "send0", "mask1", "send1", "mask2", "send2", "rest",
-    "f2", "scores", "f3", "weight", "gn0", "f4", "relay0", "relay1", "relay2", "mix",
-    "w0_0", "part_far", "part_next", "part_prev", "w1_0", "near", "w0_1", "w0_2", "gn1", "gn2", "own", "w1_1", "w1_2", "w2_0",
-    "far0", "far1", "far2", "w0_3", "fill", "b1", "w1_3", "w2_1", "w2_2", "w3_0", "add0", "add1", "add2", "b2", "local0", "w2_3", "w4_0", "w3_1", "w3_2",
-    "local1", "b3", "local2", "w3_3", "w4_1", "w4_2", "w5_0", "b4", "back_end", "w4_3", "w5_1", "w5_2", "w6_0", "w6_1", "w6_2", "fin0", "w5_3", "fin1", "fin2", "w6_3",
+    "go", "mask0", "states", "meet", "f1", "send0", "go_rest", "mask1", "send1", "mask2", "send2", "rest", "f2", "scores", "f3", "weight", "gn0",
+    "relay0", "relay1", "relay2", "f4", "mix", "w0_0", "part_far", "part_next", "w1_0", "near", "w0_1", "w0_2", "gn1", "w1_1", "w1_2", "gn2", "own", "w2_0",
+    "far0", "far1", "far2", "w0_3", "fill", "b1", "part_prev", "w2_1", "w2_2", "w3_0", "w1_3", "local0", "add0", "b2", "add1", "add2", "w3_1", "w3_2", "w4_0", "w2_3",
+    "local1", "b3", "w4_1", "w4_2", "w5_0", "w3_3", "local2", "w6_0", "b4", "back_end", "w5_1", "w4_3", "w5_2", "w6_1", "w6_2", "fin0", "w5_3", "fin1", "fin2", "w6_3",
 )
 
 
@@ -151,18 +150,18 @@
 
     lax.fori_loop(1, N_ROW, greet, 0)
 
+    rest = pl.ds(SPAN, ROWS - SPAN)
     loads = [
         pltpu.make_async_copy(a, b, load_sem.at[i])
         for i, (a, b) in enumerate(
             (
-                (go_hbm, go), (k_hbm, k), (v_hbm, v), (q_hbm, q), (w_hbm, w),
-                (seed_hbm, seed_ref),
+                (go_hbm.at[rows(0)], go.at[rows(0)]), (k_hbm, k), (v_hbm, v), (q_hbm, q),
+                (w_hbm, w), (seed_hbm, seed_ref), (go_hbm.at[rest], go.at[rest]),
             )
         )
     ]
-    loads[5].start()
-    for load in loads[:5]:
-        load.start()
+    for i in (5, 0, 1, 2, 6):
+        loads[i].start()
 
     def ag_own(b, way, late):
         part = half_rows(b, 1 - way if late else way)
@@ -181,7 +180,7 @@
     first_row = seq * ROWS
     first_column = y * WIDTH
     features = first_column + lax.broadcasted_iota(jnp.int32, (1, WIDTH), 1)
-    TILE = 16
+    TILE = 32
 
     def mask(b):
         seed = seed_ref[0]
@@ -498,6 +497,12 @@
     def do_far(b):
         arrive(gp.at[3, rows(b)], ag_r.at[4 + b])
 
+    def do_go():
+        loads[5].wait()
+        loads[0].wait()
+        loads[3].start()
+        loads[4].start()
+
     def do_states():
         loads[1].wait()
         loads[2].wait()
@@ -521,7 +526,8 @@
         blocks(back_end)
 
     steps = {
-        "go": lambda: (loads[5].wait(), loads[0].wait()),
+        "go": do_go,
+        "go_rest": loads[6].wait,
         "weight": loads[4].wait,
         "meet": lambda: pl.semaphore_wait(barrier, 2 + N_ROW - 1 + N_Z - 1),
         "states": do_states,
@@ -577,13 +583,13 @@
 
 def write_out(*refs):
     sources, targets, done = refs[:5], refs[5:10], refs[10]
-    copies = [
-        pltpu.make_async_copy(a, b, done.at[i]) for i, (a, b) in enumerate(zip(sources, targets))
-    ]
-    for copy in copies:
-        copy.start()
-    for copy in copies:
-        copy.wait()
+    for i, (source, target) in enumerate(zip(sources, targets)):
+        part = source.shape[0] // 4
+        for n in range(4):
+            at = pl.ds(n * part, part)
+            pltpu.make_async_copy(source.at[at], target.at[at], done.at[i]).start()
+    for i, (source, target) in enumerate(zip(sources, targets)):
+        pltpu.make_async_copy(source, target, done.at[i]).wait()
 
 
 def local(queries, attn_keys, attn_values, out_weight, grad_out, drop_seed):
@@ -631,7 +637,7 @@
         vmem((4, 8, 16, 256), BF16),
         vmem((4, 4, 64, 512), BF16),
         vmem((4, 4, 64, 512), BF16),
-        dma((6,)),
+        dma((7,)),
         dma((2,)), dma((7,)),
         dma((2,)), dma((6,)),
         dma((2, 3)), dma((2, 3)),

time: 72.3 us -> 71 us (0.982)
  Pallas kernels: 70.9 us -> 69.6 us
    pallas_call x1, Pallas kernels: 68.5 us -> 67.2 us  [local(): pl.pallas_call(kernel, out_shape=[vmem(square, BF16)] * 4 + [vmem((8, 64,...]
where the time goes in v4:
time: 71 us; the launch traced here: 70.9 us
  Pallas kernels  69.6 us (98%)
  between operations  1.29 us (2%)
    pallas_call x1, Pallas kernels, local(): pl.pallas_call(kernel, out_shape=[vmem(square, BF16)] * 4 + [vmem((8, 64,...  67.2 us
    pallas_call x1, Pallas kernels, local(): pl.pallas_call(write_out, out_shape=[jax.ShapeDtypeStruct(square, BF16)]...  2.37 us

profile of v4, /device:TPU:1, one launch (start us, length us, event | category | flops | bytes accessed | tf_op | source)
XLA Modules:
  0.0 70.9 jit_solution(3882784863795067586)
XLA Ops:
  1.3 67.2 %layer.1 = (bf16[768,512]{1,0:T(8,128)(2,1)S(1)}, bf16[768,512]{1,0:T(8,128)(2,1)S(1)}, bf16[768,512]{1,0:T(8,128)(2,1)S(1)}, bf16[768,512]{1,0:T(8,128)(2,1)S(1)}, bf16[8,64,2048]{2,1,0:T(8,128)(2,1)S(1)}) custom-call(s32[1]{0:T(128)S(6)} %copy.11.seed_hbm, bf16[768,512]{1,0:T(8,128)(2,1)} %q_hbm.1, bf16[768,512]{1,0:T(8,128)(2,1)} %k_hbm.1, ...), custom_call_target="tpu_custom_call" | custom-call | flops 7000000000 | bytes 11000000 | tf_op jit(solution)/shard_map/layer/pallas_call | solution.py:647
  68.5 2.4 %write_out.1 = (bf16[768,512]{1,0:T(8,128)(2,1)}, bf16[768,512]{1,0:T(8,128)(2,1)}, bf16[768,512]{1,0:T(8,128)(2,1)}, bf16[768,512]{1,0:T(8,128)(2,1)}, bf16[8,64,2048]{2,1,0:T(8,128)(2,1)}) custom-call(bf16[768,512]{1,0:T(8,128)(2,1)S(1)} %get-tuple-element.15.refs_0_, bf16[768,512]{1,0:T(8,128)(2,1)S(1)} %get-tuple-element.16.refs_1_, ...), custom_call_target="tpu_custom_call" | custom-call | tf_op jit(solution)/shard_map/write_out/pallas_call | solution.py:661

commit v5 on v4

--- a/solution.py
+++ b/solution.py
@@ -118,7 +118,7 @@
 
     def loop(count, act):
         def step(i, _):
-            act(i)
+            act((i + count // 2 - 2) % (count - 1) + 1)
             return 0
 
         lax.fori_loop(1, count, step, 0)

time: 71 us -> 70.3 us (level)
  no operation moved by 1% of the time
where the time goes in v5:
time: 70.3 us; the launch traced here: 70.2 us
  Pallas kernels  68.9 us (98%)
  between operations  1.29 us (2%)
    pallas_call x1, Pallas kernels, local(): pl.pallas_call(kernel, out_shape=[vmem(square, BF16)] * 4 + [vmem((8, 64,...  66.5 us
    pallas_call x1, Pallas kernels, local(): pl.pallas_call(write_out, out_shape=[jax.ShapeDtypeStruct(square, BF16)]...  2.37 us

profile of v5, /device:TPU:1, one launch (start us, length us, event | category | flops | bytes accessed | tf_op | source)
XLA Modules:
  0.0 70.2 jit_solution(6075835775294122454)
XLA Ops:
  1.3 66.5 %layer.1 = (bf16[768,512]{1,0:T(8,128)(2,1)S(1)}, bf16[768,512]{1,0:T(8,128)(2,1)S(1)}, bf16[768,512]{1,0:T(8,128)(2,1)S(1)}, bf16[768,512]{1,0:T(8,128)(2,1)S(1)}, bf16[8,64,2048]{2,1,0:T(8,128)(2,1)S(1)}) custom-call(s32[1]{0:T(128)S(6)} %copy.11.seed_hbm, bf16[768,512]{1,0:T(8,128)(2,1)} %q_hbm.1, bf16[768,512]{1,0:T(8,128)(2,1)} %k_hbm.1, ...), custom_call_target="tpu_custom_call" | custom-call | flops 7000000000 | bytes 11000000 | tf_op jit(solution)/shard_map/layer/pallas_call | solution.py:647
  67.8 2.4 %write_out.1 = (bf16[768,512]{1,0:T(8,128)(2,1)}, bf16[768,512]{1,0:T(8,128)(2,1)}, bf16[768,512]{1,0:T(8,128)(2,1)}, bf16[768,512]{1,0:T(8,128)(2,1)}, bf16[8,64,2048]{2,1,0:T(8,128)(2,1)}) custom-call(bf16[768,512]{1,0:T(8,128)(2,1)S(1)} %get-tuple-element.15.refs_0_, bf16[768,512]{1,0:T(8,128)(2,1)S(1)} %get-tuple-element.16.refs_1_, ...), custom_call_target="tpu_custom_call" | custom-call | tf_op jit(solution)/shard_map/write_out/pallas_call | solution.py:661
